TPU v7x, 512 devices: a whole 4x8x8 slice. The times are simulated.
512 devices in a mesh: replica: 8 (over z), fsdp: 64 (over y, x, core).
Axes of the slice: x: 4, y: 8, z: 8, core: 2. Of those that a mesh axis runs over, the one named last changes fastest.
Arguments:
- grad_partials: float32 [8, 5120, 7168], P('replica', 'fsdp'), may hold values from -3300 to 3300
- momentum: float32 [5120, 7168], P('fsdp', 'replica'), may hold values from -4600 to 4600
Outputs:
- update: float32 [5120, 7168], P('fsdp', 'replica')
- momentum_next: float32 [5120, 7168], P('fsdp', 'replica')
All inputs are finite; a program needn't handle non-finite values.
Results may differ from a plain program's by a relative error of at most 0.0003.
Values sent between devices are 32-bit elements; how exact they have to be, the bound alone decides.
No kernel may reach another device: no remote copies, remote signals or barrier semaphores. Data moves between devices by JAX's collectives and lax.ppermute only.
A program may use at most 64 MiB of HBM per device.

v0:
```python
import math

import jax
import jax.numpy as jnp
from jax import lax
from jax.sharding import PartitionSpec as P

COLS = 5120
HEAD_DIM = 128
ITERS = 5


quintic_a = 3.4445
quintic_b = -4.775
quintic_c = 2.0315
beta_decay = 0.95
norm_eps = 1e-07
highest = lax.Precision.HIGHEST


def local_gram(current):
    return jnp.einsum(
        "cka,ckb->kab", current, current, precision=highest, preferred_element_type=jnp.float32
    )


def advance(current, square):
    polynomial = quintic_b * square + quintic_c * jnp.einsum(
        "kab,kbd->kad", square, square, precision=highest, preferred_element_type=jnp.float32
    )
    return quintic_a * current + jnp.einsum(
        "cka,kab->ckb", current, polynomial, precision=highest, preferred_element_type=jnp.float32
    )


def whole_heads(gathered):
    totals = jnp.sum(gathered * gathered, axis=(0, 2))
    current = gathered / (jnp.sqrt(totals) + norm_eps)[None, :, None]
    for iteration in range(ITERS):
        current = advance(current, local_gram(current))
    return current


def owner_work(received):
    return whole_heads(received[:, 0])[:, None]


def on_device(grad_partials, momentum):
    grad_sum = lax.psum_scatter(grad_partials[0], "replica", scatter_dimension=1, tiled=True)
    momentum_next = beta_decay * momentum + grad_sum
    blended = grad_sum + beta_decay * momentum_next
    col_count, row_count = blended.shape
    head_count = row_count // HEAD_DIM
    stacked = blended.reshape(col_count, head_count, HEAD_DIM)
    owners = lax.axis_size("fsdp")
    per_owner = -(-head_count // owners)
    padded = jnp.pad(stacked, ((0, 0), (0, per_owner * owners - head_count), (0, 0)))
    padded = padded.reshape(col_count, owners, per_owner, HEAD_DIM)
    worked = owner_work(lax.all_to_all(padded, "fsdp", split_axis=1, concat_axis=0, tiled=True))
    returned = lax.all_to_all(worked, "fsdp", split_axis=0, concat_axis=1, tiled=True)
    orthogonal = returned.reshape(col_count, owners * per_owner, HEAD_DIM)[:, :head_count]
    factor = 0.2 * math.sqrt(max(HEAD_DIM, COLS))
    update = factor * orthogonal.reshape(col_count, row_count)
    return (update, momentum_next)


def solution(mesh):
    return jax.shard_map(
        on_device,
        mesh=mesh,
        in_specs=(P("replica", "fsdp", None), P("fsdp", "replica")),
        out_specs=(P("fsdp", "replica"), P("fsdp", "replica")),
        check_vma=False,
    )
```

profile of v0, /device:TPU:1, one launch (start us, length us, event | category | flops | bytes accessed | tf_op | source)
XLA Modules:
  0.0 255.2 jit_solution(10417124586198476309)
XLA Ops:
  7.2 0.7 reduce-scatter.2.cloned.1.call-update
  7.9 50.5 %reduce-scatter.2.cloned.1.call-done = f32[80,896]{1,0:T(8,128)} async-done(((f32[80,7168]{1,0:T(8,128)}), f32[80,896]{1,0:T(8,128)}) %reduce-scatter.2.cloned.1.call-update) | async-done | bytes 286736 | tf_op jit(solution)/shard_map/reduce_scatter | solution.py:49
  58.4 1.8 multiply_add_fusion
  60.3 0.3 pad_bitcast_fusion
  60.6 1.5 copy.10
  62.1 77.2 %all_to_all.24 = f32[80,64,1,128]{3,0,2,1:T(8,128)S(1)} all-to-all(f32[80,64,1,128]{3,0,2,1:T(8,128)S(1)} %copy.10), channel_id=1, replica_groups=mesh['replica'=8,'fsdp'=64] {'fsdp'}, dimensions={1} | all-to-all | bytes 5242880 | tf_op jit(solution)/shard_map/all_to_all | solution.py:59
  139.3 1.3 multiply_reduce_fusion
  141.3 2.7 %broadcast_multiply_fusion = (f32[80,64,1,128]{3,0,1,2:T(8,128)}, f32[80,64,1,128]{3,0,1,2:T(8,128)}) fusion(f32[]{:T(128)S(6)} %add.51, f32[80,64,1,128]{3,0,2,1:T(8,128)S(1)} %all_to_all.24), kind=kLoop, calls=%fused_computation.28 | loop fusion | flops 1310720 | bytes 7864324 | tf_op jit(solution)/shard_map/mul | solution.py:31
  144.0 3.4 %copy.12 = f32[5120,1,128]{0,2,1:T(8,128)} copy(f32[5120,1,128]{2,0,1:T(8,128)} %bitcast.105) | data formatting | bytes 5242880 | tf_op jit(solution)/shard_map/mul | solution.py:31
  147.4 4.3 %fusion.25 = f32[128,128]{1,0:T(8,128)S(1)} fusion(f32[80,64,1,128]{3,0,1,2:T(8,128)S(1)} %copy-done), kind=kOutput, calls=%fused_computation.39 | convolution fusion | flops 1006632960 | bytes 2686976 | tf_op jit(solution)/shard_map/cka,ckb->kab/dot_general | solution.py:22
  151.7 0.2 fusion.24
  151.9 2.6 %fusion = f32[5120,1,128]{0,2,1:T(8,128)S(1)} fusion(f32[5120,1,128]{0,2,1:T(8,128)S(1)} %copy-done.1, f32[128,128]{1,0:T(8,128)S(1)} %fusion.24, f32[5120,128]{1,0:T(8,128)S(1)} %bitcast.104), kind=kOutput, calls=%fused_computation.5 | convolution fusion | flops 1007288320 | bytes 7929856 | tf_op jit(solution)/shard_map/cka,kab->ckb/dot_general | solution.py:31
  154.5 2.2 fusion.18
  156.9 2.7 %fusion.1 = f32[5120,1,128]{0,2,1:T(8,128)S(1)} fusion(f32[128,128]{1,0:T(8,128)S(1)} %fusion.23, f32[5120,1,128]{0,2,1:T(8,128)S(1)} %fusion), kind=kOutput, calls=%fused_computation.6 | convolution fusion | flops 1007943680 | bytes 5308416 | tf_op jit(solution)/shard_map/cka,kab->ckb/dot_general | solution.py:31
  159.6 2.4 fusion.15
  162.3 2.7 %fusion.2 = f32[5120,1,128]{0,2,1:T(8,128)S(1)} fusion(f32[128,128]{1,0:T(8,128)S(1)} %fusion.22, f32[5120,1,128]{0,2,1:T(8,128)S(1)} %fusion.1), kind=kOutput, calls=%fused_computation.7 | convolution fusion | flops 1007943680 | bytes 5308416 | tf_op jit(solution)/shard_map/cka,kab->ckb/dot_general | solution.py:31
  165.0 2.2 fusion.12
  167.4 2.7 %fusion.3 = f32[5120,1,128]{0,2,1:T(8,128)S(1)} fusion(f32[128,128]{1,0:T(8,128)S(1)} %fusion.21, f32[5120,1,128]{0,2,1:T(8,128)S(1)} %fusion.2), kind=kOutput, calls=%fused_computation.8 | convolution fusion | flops 1007943680 | bytes 5308416 | tf_op jit(solution)/shard_map/cka,kab->ckb/dot_general | solution.py:31
  170.1 2.2 fusion.9
  172.3 0.2 fusion.20
  172.5 2.9 %fusion.5 = f32[5120,1,1,128]{0,3,2,1:T(8,128)S(1)} fusion(f32[128,128]{1,0:T(8,128)S(1)} %fusion.20, f32[5120,1,128]{0,2,1:T(8,128)S(1)} %fusion.3), kind=kOutput, calls=%fused_computation.10 | convolution fusion | flops 1007943680 | bytes 5308416 | tf_op jit(solution)/shard_map/cka,kab->ckb/dot_general | solution.py:31
  175.4 3.9 %copy.13 = f32[5120,1,1,128]{3,2,1,0:T(1,128)} copy(f32[5120,1,1,128]{0,3,2,1:T(8,128)S(1)} %fusion.5) | data formatting | bytes 5242880 | tf_op jit(solution)/shard_map/broadcast_in_dim | solution.py:45
  179.3 68.4 %all_to_all.25 = f32[5120,1,1,128]{3,2,1,0:T(1,128)S(1)} all-to-all(f32[5120,1,1,128]{3,2,1,0:T(1,128)} %copy.13), channel_id=1, replica_groups=mesh['replica'=8,'fsdp'=64] {'fsdp'}, dimensions={0} | all-to-all | bytes 5242880 | tf_op jit(solution)/shard_map/all_to_all | solution.py:60
  247.6 0.7 copy_bitcast_fusion
  (9 shorter events, 0.7 us)
Async XLA Ops:
  7.2 51.2 %reduce-scatter.2.cloned.1.call-start = ((), (), s32[]{:S(2)}) async-start(), calls=%async_computation.3 | async-start | bytes 2580480 | tf_op jit(solution)/shard_map/reduce_scatter | solution.py:49
  144.0 3.4 %copy-start = (f32[80,64,1,128]{3,0,1,2:T(8,128)S(1)}, f32[80,64,1,128]{3,0,1,2:T(8,128)}, u32[]{:S(2)}) copy-start(f32[80,64,1,128]{3,0,1,2:T(8,128)} %get-tuple-element.3) | copy-start | bytes 7864324
  147.4 4.5 %copy-start.1 = (f32[5120,1,128]{0,2,1:T(8,128)S(1)}, f32[5120,1,128]{0,2,1:T(8,128)}, u32[]{:S(2)}) copy-start(f32[5120,1,128]{0,2,1:T(8,128)} %copy.12) | copy-start | bytes 7864324
Sparse Core Ops, SparseCore 0:
  10.9 47.5 reduce-scatter.1
where the time goes:
time: 255 us
  blocking collectives  146 us (57%)
  waiting for transfers between devices  51.2 us (20%)
  matrix products  27.8 us (11%)
  between operations  14.9 us (6%)
  local copies, waits for them, and re-layouts  9.19 us (4%)
  other arithmetic  6.54 us (3%)
    all_to_all x1, blocking collectives, on_device(): lax.all_to_all(padded, 'fsdp', split_axis=1, concat_axis=0, tiled=True)  77.2 us
    all_to_all x1, blocking collectives, on_device(): lax.all_to_all(worked, 'fsdp', split_axis=0, concat_axis=1, tiled=True)  68.4 us
    reduce_scatter x1, waiting for transfers between devices, on_device(): lax.psum_scatter(grad_partials[0], 'replica', scatter_dimension=1, tiled=...  50.5 us
    dot_general x5, matrix products, advance(): jnp.einsum('cka,kab->ckb', current, polynomial, precision=highest, prefer...  13.5 us
    dot_general x5, matrix products, local_gram(): jnp.einsum('cka,ckb->kab', current, current, precision=highest, preferred...  13.3 us
  transfers between devices with their start and end apart: 1, of which 1 were waited for; matrix products, arithmetic and copies ran while one was open for 0% of the time, Pallas kernels for 0%

commit v1 on v0

v1 whole, which is shorter than its diff:
```python
import functools
import math

import jax
import jax.numpy as jnp
from jax import lax
from jax.experimental import pallas as pl
from jax.experimental.pallas import tpu as pltpu
from jax.sharding import Mesh, PartitionSpec as P

COLS = 5120
HEAD_DIM = 128
HALF = HEAD_DIM // 2
PACKED = HALF + 8
ITERS = 5

quintic_a = 3.4445
quintic_b = -4.775
quintic_c = 2.0315
beta_decay = 0.95
norm_eps = 1e-07
highest = lax.Precision.HIGHEST

COLUMN_AXES = ("y", "x", "core")
OWNERS = ("x", "core")


def iotas(rows):
    shape = (rows, HEAD_DIM)
    return lax.broadcasted_iota(jnp.int32, shape, 0), lax.broadcasted_iota(jnp.int32, shape, 1)


def pack(full):
    i, j = iotas(HALF)
    body = jnp.where(j > i, full[:HALF], pltpu.roll(full[HALF:], HALF, 1))
    i, j = iotas(HEAD_DIM)
    diagonal = jnp.sum(jnp.where(i == j, full, 0.0), axis=0, keepdims=True)
    return body, jnp.broadcast_to(diagonal, (8, HEAD_DIM))


def unpack(packed):
    i, j = iotas(HALF)
    body = packed[:HALF]
    top = jnp.where(j > i, body, 0.0)
    bottom = pltpu.roll(jnp.where(j < i, body, 0.0), HALF, 1)
    triangle = jnp.concatenate([top, bottom], axis=0)
    i, j = iotas(HEAD_DIM)
    diagonal = jnp.broadcast_to(packed[HALF : HALF + 1], (HEAD_DIM, HEAD_DIM))
    return jnp.where(i == j, diagonal, triangle + triangle.T)


def dot(a, b, contract=((1,), (0,))):
    return lax.dot_general(
        a, b, (contract, ((), ())), precision=highest, preferred_element_type=jnp.float32
    )


def momentum_and_gram(own_ref, right_ref, left_ref, momentum_ref, next_ref, blended_ref, gram_ref):
    grad_sum = own_ref[...] + right_ref[...] + left_ref[...]
    momentum_next = beta_decay * momentum_ref[...] + grad_sum
    next_ref[...] = momentum_next
    blended = grad_sum + beta_decay * momentum_next
    blended_ref[...] = blended
    heads = blended.shape[1] // HEAD_DIM
    for h in range(gram_ref.shape[0]):
        if h < heads:
            part = blended[:, h * HEAD_DIM : (h + 1) * HEAD_DIM]
            body, diagonal = pack(dot(part, part, ((0,), (0,))))
            gram_ref[h, :HALF] = body
            gram_ref[h, HALF:] = diagonal
        else:
            gram_ref[h] = jnp.zeros_like(gram_ref[h])


def newton_schulz(parts_ref, out_ref):
    packed = jnp.sum(parts_ref[...], axis=0)
    total = jnp.sum(packed[HALF : HALF + 1])
    scale = 1.0 / (jnp.sqrt(total) + norm_eps)
    square = unpack(packed) * scale * scale
    i, j = iotas(HEAD_DIM)
    eye = jnp.where(i == j, quintic_a, 0.0)
    product = None
    for iteration in range(ITERS):
        polynomial = eye + quintic_b * square + quintic_c * dot(square, square)
        product = polynomial if product is None else dot(product, polynomial)
        if iteration < ITERS - 1:
            square = dot(dot(square, polynomial), polynomial)
    factor = 0.2 * math.sqrt(max(HEAD_DIM, COLS))
    body, diagonal = pack(product * (factor * scale))
    out_ref[:HALF] = body
    out_ref[HALF:] = diagonal


def apply(blended_ref, product_ref, out_ref):
    for h in range(out_ref.shape[1] // HEAD_DIM):
        cols = slice(h * HEAD_DIM, (h + 1) * HEAD_DIM)
        out_ref[:, cols] = dot(blended_ref[:, cols], unpack(product_ref[h]))


def call(body, out_shape, *args):
    return pl.pallas_call(
        body,
        out_shape=out_shape,
        compiler_params=pltpu.CompilerParams(vmem_limit_bytes=32 * 1024 * 1024),
    )(*args)


def f32(*shape):
    return jax.ShapeDtypeStruct(shape, jnp.float32)


def replica_sums(grad):
    size, me = lax.axis_size("replica"), lax.axis_index("replica")
    width = grad.shape[1] // size

    def chunk(k):
        return lax.dynamic_slice(grad, (0, lax.rem(me + k, size) * width), (grad.shape[0], width))

    def send(value, step):
        return lax.ppermute(value, "replica", [(i, (i + step) % size) for i in range(size)])

    far, half = chunk(size // 2), width // 256 * 128
    right = send(far[:, :half], 1)
    left = send(far[:, half:], -1)
    near_right, near_left = chunk(3), chunk(5)
    right = jnp.concatenate([near_right[:, :half] + right, near_right[:, half:]], axis=1)
    left = jnp.concatenate([near_left[:, :half], near_left[:, half:] + left], axis=1)
    for k in (2, 1, 0):
        right, left = send(right, 1), send(left, -1)
        if k:
            right, left = chunk(k) + right, chunk(size - k) + left
    return chunk(0), right, left


def on_device(grad_partials, momentum):
    own, right, left = replica_sums(grad_partials[0])
    cols, rows = momentum.shape
    heads = rows // HEAD_DIM
    owners = lax.axis_size(OWNERS)
    momentum_next, blended, gram = call(
        momentum_and_gram,
        (f32(cols, rows), f32(cols, rows), f32(owners, PACKED, HEAD_DIM)),
        own,
        right,
        left,
        momentum,
    )
    parts = lax.all_to_all(gram, OWNERS, split_axis=0, concat_axis=0, tiled=True)
    part = jnp.sum(parts, axis=0)
    parts = jnp.broadcast_to(part[None], (lax.axis_size("y"), PACKED, HEAD_DIM))
    parts = lax.all_to_all(parts, "y", split_axis=0, concat_axis=0, tiled=True)
    product = call(newton_schulz, f32(PACKED, HEAD_DIM), parts)
    products = jnp.broadcast_to(product[None], (owners, PACKED, HEAD_DIM))
    products = lax.all_to_all(products, OWNERS, split_axis=0, concat_axis=0, tiled=True)
    update = call(apply, f32(cols, rows), blended, products)
    return update, momentum_next


def solution(mesh):
    fine = Mesh(mesh.devices.reshape(8, 8, 4, 2), ("replica", *COLUMN_AXES))
    return jax.shard_map(
        on_device,
        mesh=fine,
        in_specs=(P("replica", COLUMN_AXES, None), P(COLUMN_AXES, "replica")),
        out_specs=(P(COLUMN_AXES, "replica"), P(COLUMN_AXES, "replica")),
        check_vma=False,
    )
```

time: 255 us -> 110 us (0.43)
  blocking collectives: 146 us -> 46.7 us
  waiting for transfers between devices: 51.2 us -> 14 us
  starting transfers between devices: 0.04 us -> 35.4 us
  matrix products: 27.8 us -> 0 us
  between operations: 14.9 us -> 0.86 us
  local copies, waits for them, and re-layouts: 9.19 us -> 2.87 us
  Pallas kernels: 0 us -> 5.65 us
    all_to_all x2 -> x3, blocking collectives: 146 us -> 46.7 us  [the longest x1 17.7 us: on_device(): parts = lax.all_to_all(parts, 'y', split_axis=0, concat_axis=0, tiled=True)]
    reduce_scatter x1 -> x0, waiting for transfers between devices: 50.5 us -> none  [on_device(): lax.psum_scatter(grad_partials[0], 'replica', scatter_dimension=1, tiled=...]
    ppermute x0 -> x8, starting transfers between devices: none -> 35.4 us  [send(): lax.ppermute(value, 'replica', [(i, (i + step) % size) for i in range(siz...]
    dot_general x15 -> x0, matrix products: 27.8 us -> none  [the longest x5 13.5 us: advance(): jnp.einsum('cka,kab->ckb', current, polynomial, precision=highest, prefer...]
    ppermute x0 -> x8, waiting for transfers between devices: none -> 14 us  [send(): lax.ppermute(value, 'replica', [(i, (i + step) % size) for i in range(siz...]
    pallas_call x0 -> x3, Pallas kernels: none -> 5.65 us  [call(): pl.pallas_call(body, out_shape=out_shape, compiler_params=pltpu.CompilerP...]
    broadcast_in_dim x1 -> x2, local copies, waits for them, and re-layouts: 3.9 us -> 0.04 us  [the longest x1 0.02 us: on_device(): parts = jnp.broadcast_to(part[None], (lax.axis_size('y'), PACKED, HEAD_DIM))]
    mul x2 -> x0, other arithmetic: 3.47 us -> none  [the longest x1 2.73 us: advance(): quintic_a * current]
  transfers between devices with their start and end apart: 1 -> 8, of which waited for: 1 -> 6; matrix products, arithmetic and copies ran while one was open for 0% -> 3% of each run, Pallas kernels for 0% -> 0%
where the time goes in v1:
time: 110 us
  blocking collectives  46.7 us (42%)
  starting transfers between devices  35.4 us (32%)
  waiting for transfers between devices  14 us (13%)
  Pallas kernels  5.65 us (5%)
  other arithmetic  4.45 us (4%)
  local copies, waits for them, and re-layouts  2.87 us (3%)
    ppermute x8, starting transfers between devices, send(): lax.ppermute(value, 'replica', [(i, (i + step) % size) for i in range(siz...  35.4 us
    all_to_all x1, blocking collectives, on_device(): parts = lax.all_to_all(parts, 'y', split_axis=0, concat_axis=0, tiled=True)  17.7 us
    all_to_all x1, blocking collectives, on_device(): lax.all_to_all(gram, OWNERS, split_axis=0, concat_axis=0, tiled=True)  16.8 us
    ppermute x8, waiting for transfers between devices, send(): lax.ppermute(value, 'replica', [(i, (i + step) % size) for i in range(siz...  14 us
    all_to_all x1, blocking collectives, on_device(): lax.all_to_all(products, OWNERS, split_axis=0, concat_axis=0, tiled=True)  12.2 us
    pallas_call x3, Pallas kernels, call(): pl.pallas_call(body, out_shape=out_shape, compiler_params=pltpu.CompilerP...  5.65 us
  transfers between devices with their start and end apart: 8, of which 6 were waited for; matrix products, arithmetic and copies ran while one was open for 3% of the time, Pallas kernels for 0%

profile of v1, /device:TPU:1, one launch (start us, length us, event | category | flops | bytes accessed | tf_op | source)
XLA Modules:
  0.0 109.9 jit_solution(17845259554069872200)
XLA Ops:
  0.7 1.5 %dynamic-slice_bitcast_fusion = (f32[80,896]{1,0:T(8,128)S(1)}, f32[80,896]{1,0:T(8,128)S(1)}, f32[80,896]{1,0:T(8,128)S(1)}, f32[80,896]{1,0:T(8,128)S(1)}) fusion(f32[1,80,7168]{2,1,0:T(8,128)} %param.2, s32[]{:T(128)S(6)} %select_n.31, s32[]{:T(128)S(6)} %select_n.28, s32[]{:T(128)S(6)} %select_n.27, s32[]{:T(128)S(6)} %select_n.24), kind=kLoop, calls=%fused_computation.6 | loop fusion | bytes 2293776 | tf_op jit(solution)/shard_map/dynamic_slice | solution.py:117
  2.8 11.5 %collective-permute-start.4 = (f32[80,512]{1,0:T(8,128)}, f32[80,512]{1,0:T(8,128)}, u32[]{:S(2)}, u32[]{:S(2)}) collective-permute-start(f32[80,512]{1,0:T(8,128)} %slice.29), channel_id=1, source_target_pairs={{0,448},{64,0},{128,64},{192,128},{256,192},{320,256},{384,320},{4... | collective-permute-start | bytes 491528 | tf_op jit(solution)/shard_map/ppermute | solution.py:120
  15.0 1.9 %collective-permute-start = (f32[80,384]{1,0:T(8,128)}, f32[80,384]{1,0:T(8,128)}, u32[]{:S(2)}, u32[]{:S(2)}) collective-permute-start(f32[80,384]{1,0:T(8,128)} %slice.25), channel_id=1, source_target_pairs={{0,64},{64,128},{128,192},{192,256},{256,320},{320,384},{384,448},... | collective-permute-start | bytes 368648 | tf_op jit(solution)/shard_map/ppermute | solution.py:120
  17.5 0.9 slice_add_fusion
  18.4 5.5 %collective-permute-start.5 = (f32[80,896]{1,0:T(8,128)S(1)}, f32[80,896]{1,0:T(8,128)S(1)}, u32[]{:S(2)}, u32[]{:S(2)}) collective-permute-start(f32[80,896]{1,0:T(8,128)S(1)} %pad_maximum_fusion.1), channel_id=1, source_target_pairs={{0,448},{64,0},{128,64},{192,128},{256,192},{320,256},{384,320},{4... | collective-permute-start | bytes 860168 | tf_op jit(solution)/shard_map/ppermute | solution.py:120
  23.9 0.9 slice_add_fusion.1
  24.8 0.7 pad_maximum_fusion
  25.6 1.9 %collective-permute-start.1 = (f32[80,896]{1,0:T(8,128)}, f32[80,896]{1,0:T(8,128)S(1)}, u32[]{:S(2)}, u32[]{:S(2)}) collective-permute-start(f32[80,896]{1,0:T(8,128)} %pad_maximum_fusion), channel_id=1, source_target_pairs={{0,64},{64,128},{128,192},{192,256},{256,320},{320,384},{384,448},... | collective-permute-start | bytes 860168 | tf_op jit(solution)/shard_map/ppermute | solution.py:120
  27.5 1.0 collective-permute-done.5
  28.5 5.3 %collective-permute-start.6 = (f32[80,896]{1,0:T(8,128)S(1)}, f32[80,896]{1,0:T(8,128)}, u32[]{:S(2)}, u32[]{:S(2)}) collective-permute-start(f32[80,896]{1,0:T(8,128)S(1)} %bitcast_add_fusion), channel_id=1, source_target_pairs={{0,448},{64,0},{128,64},{192,128},{256,192},{320,256},{384,320},{4... | collective-permute-start | bytes 860168 | tf_op jit(solution)/shard_map/ppermute | solution.py:120
  33.8 1.5 %collective-permute-done.1 = f32[80,896]{1,0:T(8,128)S(1)} collective-permute-done((f32[80,896]{1,0:T(8,128)}, f32[80,896]{1,0:T(8,128)S(1)}, u32[]{:S(2)}, u32[]{:S(2)}) %collective-permute-start.1) | collective-permute-done | bytes 286752 | tf_op jit(solution)/shard_map/ppermute | solution.py:120
  35.4 2.0 %collective-permute-done.6 = f32[80,896]{1,0:T(8,128)} collective-permute-done((f32[80,896]{1,0:T(8,128)S(1)}, f32[80,896]{1,0:T(8,128)}, u32[]{:S(2)}, u32[]{:S(2)}) %collective-permute-start.6) | collective-permute-done | bytes 286752 | tf_op jit(solution)/shard_map/ppermute | solution.py:120
  37.4 1.8 %bitcast_add_fusion.1 = (f32[80,896]{1,0:T(8,128)S(1)}, f32[80,896]{1,0:T(8,128)}) fusion(f32[80,896]{1,0:T(8,128)} %collective-permute-done.6, f32[1,80,7168]{2,1,0:T(8,128)S(1)} %copy-done.1, s32[]{:T(128)S(6)} %select_n.29, f32[80,896]{1,0:T(8,128)S(1)} %collective-permute-done.1, s32[]{:T(128)S(6)} %select_n.26), kind=kLoop, calls=%fused_computation.3 | loop fusion | flops 143360 | bytes 1720328 | tf_op jit(solution)/shard_map/add | solution.py:131
  39.1 1.9 %collective-permute-start.2 = (f32[80,896]{1,0:T(8,128)}, f32[80,896]{1,0:T(8,128)S(1)}, u32[]{:S(2)}, u32[]{:S(2)}) collective-permute-start(f32[80,896]{1,0:T(8,128)} %get-tuple-element.9), channel_id=1, source_target_pairs={{0,64},{64,128},{128,192},{192,256},{256,320},{320,384},{384,448},... | collective-permute-start | bytes 860168 | tf_op jit(solution)/shard_map/ppermute | solution.py:120
  41.1 5.5 %collective-permute-start.7 = (f32[80,896]{1,0:T(8,128)S(1)}, f32[80,896]{1,0:T(8,128)S(1)}, u32[]{:S(2)}, u32[]{:S(2)}) collective-permute-start(f32[80,896]{1,0:T(8,128)S(1)} %get-tuple-element.8), channel_id=1, source_target_pairs={{0,448},{64,0},{128,64},{192,128},{256,192},{320,256},{384,320},{4... | collective-permute-start | bytes 860168 | tf_op jit(solution)/shard_map/ppermute | solution.py:120
  46.6 2.3 %collective-permute-done.2 = f32[80,896]{1,0:T(8,128)S(1)} collective-permute-done((f32[80,896]{1,0:T(8,128)}, f32[80,896]{1,0:T(8,128)S(1)}, u32[]{:S(2)}, u32[]{:S(2)}) %collective-permute-start.2) | collective-permute-done | bytes 286752 | tf_op jit(solution)/shard_map/ppermute | solution.py:120
  48.9 1.9 %collective-permute-start.3 = (f32[80,896]{1,0:T(8,128)S(1)}, f32[80,896]{1,0:T(8,128)S(1)}, u32[]{:S(2)}, u32[]{:S(2)}) collective-permute-start(f32[80,896]{1,0:T(8,128)S(1)} %bitcast_add_fusion.3), channel_id=1, source_target_pairs={{0,64},{64,128},{128,192},{192,256},{256,320},{320,384},{384,448},... | collective-permute-start | bytes 860168 | tf_op jit(solution)/shard_map/ppermute | solution.py:120
  50.8 6.7 %collective-permute-done.3.right_ref = f32[80,896]{1,0:T(8,128)S(1)} collective-permute-done((f32[80,896]{1,0:T(8,128)S(1)}, f32[80,896]{1,0:T(8,128)S(1)}, u32[]{:S(2)}, u32[]{:S(2)}) %collective-permute-start.3) | collective-permute-done | bytes 286752 | tf_op jit(solution)/shard_map/ppermute | solution.py:120
  57.5 0.9 shard_map.41
  58.4 16.8 %all_to_all.15 = f32[8,72,128]{2,1,0:T(8,128)S(1)} all-to-all(f32[8,72,128]{2,1,0:T(8,128)S(1)} %get-tuple-element.6), channel_id=1, replica_groups=mesh['replica'=8,'y'=8,'x'=4,'core'=2] {'x','core'}, dimensions={0} | all-to-all | bytes 589824 | tf_op jit(solution)/shard_map/all_to_all | solution.py:148
  75.3 17.7 %all_to_all.16.parts_ref = f32[8,72,128]{2,1,0:T(8,128)S(1)} all-to-all(f32[8,72,128]{2,1,0:T(8,128)S(1)} %broadcast_in_dim.4), channel_id=1, replica_groups=mesh['replica'=8,'y'=8,'x'=4,'core'=2] {'y'}, dimensions={0} | all-to-all | bytes 589824 | tf_op jit(solution)/shard_map/all_to_all | solution.py:151
  93.0 3.4 %shard_map.42 = f32[72,128]{1,0:T(8,128)S(1)} custom-call(f32[8,72,128]{2,1,0:T(8,128)S(1)} %all_to_all.16.parts_ref), custom_call_target="tpu_custom_call" | custom-call | tf_op jit(solution)/shard_map/pallas_call | solution.py:101
  96.4 12.2 %all_to_all.17.product_ref = f32[8,72,128]{2,1,0:T(8,128)S(1)} all-to-all(f32[8,72,128]{2,1,0:T(8,128)S(1)} %broadcast_in_dim.5), channel_id=1, replica_groups=mesh['replica'=8,'y'=8,'x'=4,'core'=2] {'x','core'}, dimensions={0} | all-to-all | bytes 589824 | tf_op jit(solution)/shard_map/all_to_all | solution.py:154
  108.5 1.4 %shard_map.43 = f32[80,896]{1,0:T(8,128)} custom-call(f32[80,896]{1,0:T(8,128)S(1)} %get-tuple-element.5.blended_ref, f32[8,72,128]{2,1,0:T(8,128)S(1)} %all_to_all.17.product_ref), custom_call_target="tpu_custom_call" | custom-call | tf_op jit(solution)/shard_map/pallas_call | solution.py:101
  (17 shorter events, 2.1 us)
Async XLA Ops:
  0.7 27.8 %copy-start.1 = (f32[1,80,7168]{2,1,0:T(8,128)S(1)}, f32[1,80,7168]{2,1,0:T(8,128)}, u32[]{:S(2)}) copy-start(f32[1,80,7168]{2,1,0:T(8,128)} %param.2) | copy-start | bytes 6881284
  2.8 14.7 %collective-permute-start.4 = (f32[80,512]{1,0:T(8,128)}, f32[80,512]{1,0:T(8,128)}, u32[]{:S(2)}, u32[]{:S(2)}) collective-permute-start(f32[80,512]{1,0:T(8,128)} %slice.29), channel_id=1, source_target_pairs={{0,448},{64,0},{128,64},{192,128},{256,192},{320,256},{384,320},{4... | collective-permute-start | bytes 491528 | tf_op jit(solution)/shard_map/ppermute | solution.py:120
  15.0 8.9 %collective-permute-start = (f32[80,384]{1,0:T(8,128)}, f32[80,384]{1,0:T(8,128)}, u32[]{:S(2)}, u32[]{:S(2)}) collective-permute-start(f32[80,384]{1,0:T(8,128)} %slice.25), channel_id=1, source_target_pairs={{0,64},{64,128},{128,192},{192,256},{256,320},{320,384},{384,448},... | collective-permute-start | bytes 368648 | tf_op jit(solution)/shard_map/ppermute | solution.py:120
  18.4 39.1 %copy-start = (f32[80,896]{1,0:T(8,128)S(1)}, f32[80,896]{1,0:T(8,128)}, u32[]{:S(2)}) copy-start(f32[80,896]{1,0:T(8,128)} %momentum_ref.1) | copy-start | bytes 860164
  18.4 10.0 %collective-permute-start.5 = (f32[80,896]{1,0:T(8,128)S(1)}, f32[80,896]{1,0:T(8,128)S(1)}, u32[]{:S(2)}, u32[]{:S(2)}) collective-permute-start(f32[80,896]{1,0:T(8,128)S(1)} %pad_maximum_fusion.1), channel_id=1, source_target_pairs={{0,448},{64,0},{128,64},{192,128},{256,192},{320,256},{384,320},{4... | collective-permute-start | bytes 860168 | tf_op jit(solution)/shard_map/ppermute | solution.py:120
  25.6 9.8 %collective-permute-start.1 = (f32[80,896]{1,0:T(8,128)}, f32[80,896]{1,0:T(8,128)S(1)}, u32[]{:S(2)}, u32[]{:S(2)}) collective-permute-start(f32[80,896]{1,0:T(8,128)} %pad_maximum_fusion), channel_id=1, source_target_pairs={{0,64},{64,128},{128,192},{192,256},{256,320},{320,384},{384,448},... | collective-permute-start | bytes 860168 | tf_op jit(solution)/shard_map/ppermute | solution.py:120
  28.5 8.9 %collective-permute-start.6 = (f32[80,896]{1,0:T(8,128)S(1)}, f32[80,896]{1,0:T(8,128)}, u32[]{:S(2)}, u32[]{:S(2)}) collective-permute-start(f32[80,896]{1,0:T(8,128)S(1)} %bitcast_add_fusion), channel_id=1, source_target_pairs={{0,448},{64,0},{128,64},{192,128},{256,192},{320,256},{384,320},{4... | collective-permute-start | bytes 860168 | tf_op jit(solution)/shard_map/ppermute | solution.py:120
  39.1 9.7 %collective-permute-start.2 = (f32[80,896]{1,0:T(8,128)}, f32[80,896]{1,0:T(8,128)S(1)}, u32[]{:S(2)}, u32[]{:S(2)}) collective-permute-start(f32[80,896]{1,0:T(8,128)} %get-tuple-element.9), channel_id=1, source_target_pairs={{0,64},{64,128},{128,192},{192,256},{256,320},{320,384},{384,448},... | collective-permute-start | bytes 860168 | tf_op jit(solution)/shard_map/ppermute | solution.py:120
  41.1 9.8 %collective-permute-start.7 = (f32[80,896]{1,0:T(8,128)S(1)}, f32[80,896]{1,0:T(8,128)S(1)}, u32[]{:S(2)}, u32[]{:S(2)}) collective-permute-start(f32[80,896]{1,0:T(8,128)S(1)} %get-tuple-element.8), channel_id=1, source_target_pairs={{0,448},{64,0},{128,64},{192,128},{256,192},{320,256},{384,320},{4... | collective-permute-start | bytes 860168 | tf_op jit(solution)/shard_map/ppermute | solution.py:120
  48.9 8.6 %collective-permute-start.3 = (f32[80,896]{1,0:T(8,128)S(1)}, f32[80,896]{1,0:T(8,128)S(1)}, u32[]{:S(2)}, u32[]{:S(2)}) collective-permute-start(f32[80,896]{1,0:T(8,128)S(1)} %bitcast_add_fusion.3), channel_id=1, source_target_pairs={{0,64},{64,128},{128,192},{192,256},{256,320},{320,384},{384,448},... | collective-permute-start | bytes 860168 | tf_op jit(solution)/shard_map/ppermute | solution.py:120

commit v2 on v1

--- a/solution.py
+++ b/solution.py
@@ -55,8 +55,11 @@
     )
 
 
-def momentum_and_gram(own_ref, right_ref, left_ref, momentum_ref, next_ref, blended_ref, gram_ref):
-    grad_sum = own_ref[...] + right_ref[...] + left_ref[...]
+def momentum_and_gram(*refs):
+    *term_refs, momentum_ref, next_ref, blended_ref, gram_ref = refs
+    grad_sum = term_refs[0][...]
+    for term_ref in term_refs[1:]:
+        grad_sum = grad_sum + term_ref[...]
     momentum_next = beta_decay * momentum_ref[...] + grad_sum
     next_ref[...] = momentum_next
     blended = grad_sum + beta_decay * momentum_next
@@ -112,37 +115,36 @@
 def replica_sums(grad):
     size, me = lax.axis_size("replica"), lax.axis_index("replica")
     width = grad.shape[1] // size
+    half = width // 256 * 128
 
-    def chunk(k):
-        return lax.dynamic_slice(grad, (0, lax.rem(me + k, size) * width), (grad.shape[0], width))
+    def chunk(k, start=0, stop=width):
+        return lax.dynamic_slice(
+            grad, (0, lax.rem(me + k + size, size) * width + start), (grad.shape[0], stop - start)
+        )
 
     def send(value, step):
         return lax.ppermute(value, "replica", [(i, (i + step) % size) for i in range(size)])
 
-    far, half = chunk(size // 2), width // 256 * 128
-    right = send(far[:, :half], 1)
-    left = send(far[:, half:], -1)
-    near_right, near_left = chunk(3), chunk(5)
-    right = jnp.concatenate([near_right[:, :half] + right, near_right[:, half:]], axis=1)
-    left = jnp.concatenate([near_left[:, :half], near_left[:, half:] + left], axis=1)
-    for k in (2, 1, 0):
-        right, left = send(right, 1), send(left, -1)
-        if k:
-            right, left = chunk(k) + right, chunk(size - k) + left
-    return chunk(0), right, left
+    far_right, far_left = send(chunk(4, 0, half), 2), send(chunk(4, half), -2)
+    next_right, next_left = send(chunk(3), 1), send(chunk(-3), -1)
+    right, left = send(chunk(1), 1), send(chunk(-1), -1)
+    through_right = chunk(2) + next_right
+    through_right = jnp.concatenate([through_right[:, :half] + far_right, through_right[:, half:]], axis=1)
+    through_left = chunk(-2) + next_left
+    through_left = jnp.concatenate([through_left[:, :half], through_left[:, half:] + far_left], axis=1)
+    through_right, through_left = send(through_right, 2), send(through_left, -2)
+    return chunk(0), right, left, through_right, through_left
 
 
 def on_device(grad_partials, momentum):
-    own, right, left = replica_sums(grad_partials[0])
+    terms = replica_sums(grad_partials[0])
     cols, rows = momentum.shape
     heads = rows // HEAD_DIM
     owners = lax.axis_size(OWNERS)
     momentum_next, blended, gram = call(
         momentum_and_gram,
         (f32(cols, rows), f32(cols, rows), f32(owners, PACKED, HEAD_DIM)),
-        own,
-        right,
-        left,
+        *terms,
         momentum,
     )
     parts = lax.all_to_all(gram, OWNERS, split_axis=0, concat_axis=0, tiled=True)

time: 110 us -> 99.7 us (0.906)
  waiting for transfers between devices: 14 us -> 10.6 us
  other arithmetic: 4.45 us -> 1.21 us
  blocking collectives: 46.7 us -> 43.9 us
  starting transfers between devices: 35.4 us -> 33.5 us
    ppermute x8, waiting for transfers between devices: 14 us -> 10.6 us  [send(): lax.ppermute(value, 'replica', [(i, (i + step) % size) for i in range(siz...]
    all_to_all x1, blocking collectives: 16.8 us -> 14.1 us  [on_device(): lax.all_to_all(gram, OWNERS, split_axis=0, concat_axis=0, tiled=True)]
    add x5 -> x3, other arithmetic: 3.68 us -> 1.15 us  [the longest x1 1.11 us: replica_sums(): through_left = chunk(-2) + next_left]
    ppermute x8, starting transfers between devices: 35.4 us -> 33.5 us  [send(): lax.ppermute(value, 'replica', [(i, (i + step) % size) for i in range(siz...]
    dynamic_slice x1 -> x3, local copies, waits for them, and re-layouts: 1.46 us -> 3.31 us  [chunk(): lax.dynamic_slice(grad, (0, lax.rem(me + k + size, size) * width + start)...]
    slice x4 -> x2, local copies, waits for them, and re-layouts: 1.36 us -> 0.02 us  [the longest x1 0.01 us: replica_sums(): through_right[:, half:]]
  transfers between devices with their start and end apart: 8 -> 8, of which waited for: 6 -> 2; matrix products, arithmetic and copies ran while one was open for 3% -> 3% of each run, Pallas kernels for 0% -> 0%
where the time goes in v2:
time: 99.7 us; the launch traced here: 99.2 us
  blocking collectives  43.9 us (44%)
  starting transfers between devices  33.5 us (34%)
  waiting for transfers between devices  10.6 us (11%)
  Pallas kernels  5.69 us (6%)
  local copies, waits for them, and re-layouts  3.38 us (3%)
  other arithmetic  1.21 us (1%)
    ppermute x8, starting transfers between devices, send(): lax.ppermute(value, 'replica', [(i, (i + step) % size) for i in range(siz...  33.5 us
    all_to_all x1, blocking collectives, on_device(): parts = lax.all_to_all(parts, 'y', split_axis=0, concat_axis=0, tiled=True)  17.7 us
    all_to_all x1, blocking collectives, on_device(): lax.all_to_all(gram, OWNERS, split_axis=0, concat_axis=0, tiled=True)  14.1 us
    all_to_all x1, blocking collectives, on_device(): lax.all_to_all(products, OWNERS, split_axis=0, concat_axis=0, tiled=True)  12.2 us
    ppermute x8, waiting for transfers between devices, send(): lax.ppermute(value, 'replica', [(i, (i + step) % size) for i in range(siz...  10.6 us
    pallas_call x3, Pallas kernels, call(): pl.pallas_call(body, out_shape=out_shape, compiler_params=pltpu.CompilerP...  5.69 us
    dynamic_slice x3, local copies, waits for them, and re-layouts, chunk(): lax.dynamic_slice(grad, (0, lax.rem(me + k + size, size) * width + start)...  3.31 us
  transfers between devices with their start and end apart: 8, of which 2 were waited for; matrix products, arithmetic and copies ran while one was open for 3% of the time, Pallas kernels for 0%

profile of v2, /device:TPU:1, one launch (start us, length us, event | category | flops | bytes accessed | tf_op | source)
XLA Modules:
  0.0 99.2 jit_solution(142830943643362384)
XLA Ops:
  0.7 1.4 %dynamic-slice_bitcast_fusion = (f32[80,896]{1,0:T(8,128)S(1)}, f32[80,896]{1,0:T(8,128)S(1)}, f32[80,896]{1,0:T(8,128)S(1)}, f32[80,896]{1,0:T(8,128)S(1)}, f32[80,896]{1,0:T(8,128)S(1)}) fusion(f32[1,80,7168]{2,1,0:T(8,128)} %param.2, s32[]{:T(128)S(6)} %select_n.34, s32[]{:T(128)S(6)} %select_n.31, s32[]{:T(128)S(6)} %select_n.29, s32[]{:T(128)S(6)} %select_n.28, ...), kind=kLoop, calls=%fused_computation.4 | loop fusion | bytes 2867220 | tf_op jit(solution)/shard_map/dynamic_slice | solution.py:121
  2.1 11.5 %collective-permute-start.5 = (f32[80,896]{1,0:T(8,128)S(1)}, f32[80,896]{1,0:T(8,128)S(1)}, u32[]{:S(2)}, u32[]{:S(2)}) collective-permute-start(f32[80,896]{1,0:T(8,128)S(1)} %get-tuple-element.10), channel_id=1, source_target_pairs={{0,448},{64,0},{128,64},{192,128},{256,192},{320,256},{384,320},{4... | collective-permute-start | bytes 860168 | tf_op jit(solution)/shard_map/ppermute | solution.py:126
  13.6 1.9 %collective-permute-start.2 = (f32[80,896]{1,0:T(8,128)S(1)}, f32[80,896]{1,0:T(8,128)S(1)}, u32[]{:S(2)}, u32[]{:S(2)}) collective-permute-start(f32[80,896]{1,0:T(8,128)S(1)} %get-tuple-element.11), channel_id=1, source_target_pairs={{0,64},{64,128},{128,192},{192,256},{256,320},{320,384},{384,448},... | collective-permute-start | bytes 860168 | tf_op jit(solution)/shard_map/ppermute | solution.py:126
  15.5 0.9 dynamic-slice_bitcast_fusion.6
  16.4 1.9 %collective-permute-start.3 = (f32[80,384]{1,0:T(8,128)S(1)}, f32[80,384]{1,0:T(8,128)S(1)}, u32[]{:S(2)}, u32[]{:S(2)}) collective-permute-start(f32[80,384]{1,0:T(8,128)S(1)} %dynamic-slice_bitcast_fusion.6), channel_id=1, source_target_pairs={{0,128},{64,192},{128,256},{192,320},{256,384},{320,448},{384,0},{... | collective-permute-start | bytes 368648 | tf_op jit(solution)/shard_map/ppermute | solution.py:126
  18.4 0.0 copy-start
  18.4 1.0 dynamic-slice_bitcast_fusion.5
  19.4 5.5 %collective-permute-start.6 = (f32[80,512]{1,0:T(8,128)S(1)}, f32[80,512]{1,0:T(8,128)S(1)}, u32[]{:S(2)}, u32[]{:S(2)}) collective-permute-start(f32[80,512]{1,0:T(8,128)S(1)} %dynamic-slice_bitcast_fusion.5), channel_id=1, source_target_pairs={{0,384},{64,448},{128,0},{192,64},{256,128},{320,192},{384,256},{4... | collective-permute-start | bytes 491528 | tf_op jit(solution)/shard_map/ppermute | solution.py:126
  24.8 3.4 %collective-permute-start.1 = (f32[80,896]{1,0:T(8,128)S(1)}, f32[80,896]{1,0:T(8,128)S(1)}, u32[]{:S(2)}, u32[]{:S(2)}) collective-permute-start(f32[80,896]{1,0:T(8,128)S(1)} %get-tuple-element.12), channel_id=1, source_target_pairs={{0,448},{64,0},{128,64},{192,128},{256,192},{320,256},{384,320},{4... | collective-permute-start | bytes 860168 | tf_op jit(solution)/shard_map/ppermute | solution.py:126
  28.2 0.0 collective-permute-done.5
  28.2 1.9 %collective-permute-start = (f32[80,896]{1,0:T(8,128)S(1)}, f32[80,896]{1,0:T(8,128)S(1)}, u32[]{:S(2)}, u32[]{:S(2)}) collective-permute-start(f32[80,896]{1,0:T(8,128)S(1)} %get-tuple-element.13), channel_id=1, source_target_pairs={{0,64},{64,128},{128,192},{192,256},{256,320},{320,384},{384,448},... | collective-permute-start | bytes 860168 | tf_op jit(solution)/shard_map/ppermute | solution.py:126
  30.2 1.1 %bitcast_add_fusion = (f32[80,896]{1,0:T(8,128)S(1)}, f32[80,896]{1,0:T(8,128)S(1)}) fusion(f32[80,896]{1,0:T(8,128)S(1)} %collective-permute-done.5, f32[1,80,7168]{2,1,0:T(8,128)} %param.2, s32[]{:T(128)S(6)} %select_n.33, f32[80,896]{1,0:T(8,128)S(1)} %collective-permute-done.2, s32[]{:T(128)S(6)} %select_n.30), kind=kLoop, calls=%fused_computation.2 | loop fusion | flops 143360 | bytes 1720328 | tf_op jit(solution)/shard_map/add | solution.py:133
  31.3 0.0 collective-permute-done.3
  31.4 1.9 %collective-permute-start.4 = (f32[80,896]{1,0:T(8,128)S(1)}, f32[80,896]{1,0:T(8,128)S(1)}, u32[]{:S(2)}, u32[]{:S(2)}) collective-permute-start(f32[80,896]{1,0:T(8,128)S(1)} %pad_maximum_fusion), channel_id=1, source_target_pairs={{0,128},{64,192},{128,256},{192,320},{256,384},{320,448},{384,0},{... | collective-permute-start | bytes 860168 | tf_op jit(solution)/shard_map/ppermute | solution.py:126
  33.3 0.0 collective-permute-done.6
  33.4 5.5 %collective-permute-start.7 = (f32[80,896]{1,0:T(8,128)S(1)}, f32[80,896]{1,0:T(8,128)S(1)}, u32[]{:S(2)}, u32[]{:S(2)}) collective-permute-start(f32[80,896]{1,0:T(8,128)S(1)} %pad_maximum_fusion.1), channel_id=1, source_target_pairs={{0,384},{64,448},{128,0},{192,64},{256,128},{320,192},{384,256},{4... | collective-permute-start | bytes 860168 | tf_op jit(solution)/shard_map/ppermute | solution.py:126
  38.9 7.2 %collective-permute-done.4.refs_3_ = f32[80,896]{1,0:T(8,128)S(1)} collective-permute-done((f32[80,896]{1,0:T(8,128)S(1)}, f32[80,896]{1,0:T(8,128)S(1)}, u32[]{:S(2)}, u32[]{:S(2)}) %collective-permute-start.4) | collective-permute-done | bytes 286752 | tf_op jit(solution)/shard_map/ppermute | solution.py:126
  46.1 3.4 %collective-permute-done.7.refs_4_ = f32[80,896]{1,0:T(8,128)S(1)} collective-permute-done((f32[80,896]{1,0:T(8,128)S(1)}, f32[80,896]{1,0:T(8,128)S(1)}, u32[]{:S(2)}, u32[]{:S(2)}) %collective-permute-start.7) | collective-permute-done | bytes 286752 | tf_op jit(solution)/shard_map/ppermute | solution.py:126
  49.5 0.9 shard_map.41
  50.4 14.1 %all_to_all.15 = f32[8,72,128]{2,1,0:T(8,128)S(1)} all-to-all(f32[8,72,128]{2,1,0:T(8,128)S(1)} %get-tuple-element.6), channel_id=1, replica_groups=mesh['replica'=8,'y'=8,'x'=4,'core'=2] {'x','core'}, dimensions={0} | all-to-all | bytes 589824 | tf_op jit(solution)/shard_map/all_to_all | solution.py:150
  64.6 17.7 %all_to_all.16.parts_ref = f32[8,72,128]{2,1,0:T(8,128)S(1)} all-to-all(f32[8,72,128]{2,1,0:T(8,128)S(1)} %broadcast_in_dim.4), channel_id=1, replica_groups=mesh['replica'=8,'y'=8,'x'=4,'core'=2] {'y'}, dimensions={0} | all-to-all | bytes 589824 | tf_op jit(solution)/shard_map/all_to_all | solution.py:153
  82.3 3.4 %shard_map.42 = f32[72,128]{1,0:T(8,128)S(1)} custom-call(f32[8,72,128]{2,1,0:T(8,128)S(1)} %all_to_all.16.parts_ref), custom_call_target="tpu_custom_call" | custom-call | tf_op jit(solution)/shard_map/pallas_call | solution.py:104
  85.7 12.2 %all_to_all.17.product_ref = f32[8,72,128]{2,1,0:T(8,128)S(1)} all-to-all(f32[8,72,128]{2,1,0:T(8,128)S(1)} %broadcast_in_dim.5), channel_id=1, replica_groups=mesh['replica'=8,'y'=8,'x'=4,'core'=2] {'x','core'}, dimensions={0} | all-to-all | bytes 589824 | tf_op jit(solution)/shard_map/all_to_all | solution.py:156
  97.8 1.4 %shard_map.43 = f32[80,896]{1,0:T(8,128)} custom-call(f32[80,896]{1,0:T(8,128)S(1)} %get-tuple-element.5.blended_ref, f32[8,72,128]{2,1,0:T(8,128)S(1)} %all_to_all.17.product_ref), custom_call_target="tpu_custom_call" | custom-call | tf_op jit(solution)/shard_map/pallas_call | solution.py:104
  (13 shorter events, 0.2 us)
Async XLA Ops:
  2.1 26.2 %collective-permute-start.5 = (f32[80,896]{1,0:T(8,128)S(1)}, f32[80,896]{1,0:T(8,128)S(1)}, u32[]{:S(2)}, u32[]{:S(2)}) collective-permute-start(f32[80,896]{1,0:T(8,128)S(1)} %get-tuple-element.10), channel_id=1, source_target_pairs={{0,448},{64,0},{128,64},{192,128},{256,192},{320,256},{384,320},{4... | collective-permute-start | bytes 860168 | tf_op jit(solution)/shard_map/ppermute | solution.py:126
  13.6 16.6 %collective-permute-start.2 = (f32[80,896]{1,0:T(8,128)S(1)}, f32[80,896]{1,0:T(8,128)S(1)}, u32[]{:S(2)}, u32[]{:S(2)}) collective-permute-start(f32[80,896]{1,0:T(8,128)S(1)} %get-tuple-element.11), channel_id=1, source_target_pairs={{0,64},{64,128},{128,192},{192,256},{256,320},{320,384},{384,448},... | collective-permute-start | bytes 860168 | tf_op jit(solution)/shard_map/ppermute | solution.py:126
  16.4 14.9 %collective-permute-start.3 = (f32[80,384]{1,0:T(8,128)S(1)}, f32[80,384]{1,0:T(8,128)S(1)}, u32[]{:S(2)}, u32[]{:S(2)}) collective-permute-start(f32[80,384]{1,0:T(8,128)S(1)} %dynamic-slice_bitcast_fusion.6), channel_id=1, source_target_pairs={{0,128},{64,192},{128,256},{192,320},{256,384},{320,448},{384,0},{... | collective-permute-start | bytes 368648 | tf_op jit(solution)/shard_map/ppermute | solution.py:126
  18.4 31.1 %copy-start = (f32[80,896]{1,0:T(8,128)S(1)}, f32[80,896]{1,0:T(8,128)}, u32[]{:S(2)}) copy-start(f32[80,896]{1,0:T(8,128)} %refs_5_.1) | copy-start | bytes 860164
  19.4 14.0 %collective-permute-start.6 = (f32[80,512]{1,0:T(8,128)S(1)}, f32[80,512]{1,0:T(8,128)S(1)}, u32[]{:S(2)}, u32[]{:S(2)}) collective-permute-start(f32[80,512]{1,0:T(8,128)S(1)} %dynamic-slice_bitcast_fusion.5), channel_id=1, source_target_pairs={{0,384},{64,448},{128,0},{192,64},{256,128},{320,192},{384,256},{4... | collective-permute-start | bytes 491528 | tf_op jit(solution)/shard_map/ppermute | solution.py:126
  24.8 14.0 %collective-permute-start.1 = (f32[80,896]{1,0:T(8,128)S(1)}, f32[80,896]{1,0:T(8,128)S(1)}, u32[]{:S(2)}, u32[]{:S(2)}) collective-permute-start(f32[80,896]{1,0:T(8,128)S(1)} %get-tuple-element.12), channel_id=1, source_target_pairs={{0,448},{64,0},{128,64},{192,128},{256,192},{320,256},{384,320},{4... | collective-permute-start | bytes 860168 | tf_op jit(solution)/shard_map/ppermute | solution.py:126
  28.2 10.6 %collective-permute-start = (f32[80,896]{1,0:T(8,128)S(1)}, f32[80,896]{1,0:T(8,128)S(1)}, u32[]{:S(2)}, u32[]{:S(2)}) collective-permute-start(f32[80,896]{1,0:T(8,128)S(1)} %get-tuple-element.13), channel_id=1, source_target_pairs={{0,64},{64,128},{128,192},{192,256},{256,320},{320,384},{384,448},... | collective-permute-start | bytes 860168 | tf_op jit(solution)/shard_map/ppermute | solution.py:126
  31.4 14.7 %collective-permute-start.4 = (f32[80,896]{1,0:T(8,128)S(1)}, f32[80,896]{1,0:T(8,128)S(1)}, u32[]{:S(2)}, u32[]{:S(2)}) collective-permute-start(f32[80,896]{1,0:T(8,128)S(1)} %pad_maximum_fusion), channel_id=1, source_target_pairs={{0,128},{64,192},{128,256},{192,320},{256,384},{320,448},{384,0},{... | collective-permute-start | bytes 860168 | tf_op jit(solution)/shard_map/ppermute | solution.py:126
  33.4 16.1 %collective-permute-start.7 = (f32[80,896]{1,0:T(8,128)S(1)}, f32[80,896]{1,0:T(8,128)S(1)}, u32[]{:S(2)}, u32[]{:S(2)}) collective-permute-start(f32[80,896]{1,0:T(8,128)S(1)} %pad_maximum_fusion.1), channel_id=1, source_target_pairs={{0,384},{64,448},{128,0},{192,64},{256,128},{320,192},{384,256},{4... | collective-permute-start | bytes 860168 | tf_op jit(solution)/shard_map/ppermute | solution.py:126

commit v3 on v2

--- a/solution.py
+++ b/solution.py
@@ -113,27 +113,26 @@
 
 
 def replica_sums(grad):
-    size, me = lax.axis_size("replica"), lax.axis_index("replica")
+    size, me, core = lax.axis_size("replica"), lax.axis_index("replica"), lax.axis_index("core")
     width = grad.shape[1] // size
-    half = width // 256 * 128
+    toward = 1 - 2 * lax.rem(me + core, 2)
 
-    def chunk(k, start=0, stop=width):
+    def chunk(k):
         return lax.dynamic_slice(
-            grad, (0, lax.rem(me + k + size, size) * width + start), (grad.shape[0], stop - start)
+            grad, (0, lax.rem(me + toward * k + size, size) * width), (grad.shape[0], width)
         )
 
-    def send(value, step):
-        return lax.ppermute(value, "replica", [(i, (i + step) % size) for i in range(size)])
+    def send(value, distance):
+        pairs = []
+        for i in range(size):
+            for c in range(2):
+                j = (i + distance * (1 - 2 * ((i + c) % 2))) % size
+                pairs.append((2 * i + c, 2 * j + c))
+        return lax.ppermute(value, ("replica", "core"), pairs)
 
-    far_right, far_left = send(chunk(4, 0, half), 2), send(chunk(4, half), -2)
-    next_right, next_left = send(chunk(3), 1), send(chunk(-3), -1)
-    right, left = send(chunk(1), 1), send(chunk(-1), -1)
-    through_right = chunk(2) + next_right
-    through_right = jnp.concatenate([through_right[:, :half] + far_right, through_right[:, half:]], axis=1)
-    through_left = chunk(-2) + next_left
-    through_left = jnp.concatenate([through_left[:, :half], through_left[:, half:] + far_left], axis=1)
-    through_right, through_left = send(through_right, 2), send(through_left, -2)
-    return chunk(0), right, left, through_right, through_left
+    partner = [send(chunk(k), 1) for k in (4, 3, 2, 1)]
+    others = [send(chunk(-k) + part, -k) for k, part in zip((3, 2, 1), partner)]
+    return chunk(0), partner[3], *others
 
 
 def on_device(grad_partials, momentum):

time: 99.7 us -> 96.3 us (0.966)
  waiting for transfers between devices: 10.6 us -> 15.5 us
  starting transfers between devices: 33.5 us -> 29.2 us
  blocking collectives: 43.9 us -> 41.5 us
  local copies, waits for them, and re-layouts: 3.38 us -> 1.5 us
    ppermute x8 -> x7, waiting for transfers between devices: 10.6 us -> 15.5 us  [send(): return lax.ppermute(value, ('replica', 'core'), pairs)]
    ppermute x8 -> x7, starting transfers between devices: 33.5 us -> 29.2 us  [send(): return lax.ppermute(value, ('replica', 'core'), pairs)]
    all_to_all x1, blocking collectives: 14.1 us -> 11.6 us  [on_device(): lax.all_to_all(gram, OWNERS, split_axis=0, concat_axis=0, tiled=True)]
    dynamic_slice x3 -> x1, local copies, waits for them, and re-layouts: 3.31 us -> 1.45 us  [chunk(): lax.dynamic_slice(grad, (0, lax.rem(me + toward * k + size, size) * width...]
  transfers between devices with their start and end apart: 8 -> 7, of which waited for: 2 -> 4; matrix products, arithmetic and copies ran while one was open for 3% -> 1% of each run, Pallas kernels for 0% -> 0%
where the time goes in v3:
time: 96.3 us; the launch traced here: 95.5 us
  blocking collectives  41.5 us (43%)
  starting transfers between devices  29.2 us (30%)
  waiting for transfers between devices  15.5 us (16%)
  Pallas kernels  5.68 us (6%)
  local copies, waits for them, and re-layouts  1.5 us (2%)
  other arithmetic  1.25 us (1%)
    ppermute x7, starting transfers between devices, send(): return lax.ppermute(value, ('replica', 'core'), pairs)  29.2 us
    all_to_all x1, blocking collectives, on_device(): parts = lax.all_to_all(parts, 'y', split_axis=0, concat_axis=0, tiled=True)  17.7 us
    ppermute x7, waiting for transfers between devices, send(): return lax.ppermute(value, ('replica', 'core'), pairs)  15.5 us
    all_to_all x1, blocking collectives, on_device(): lax.all_to_all(products, OWNERS, split_axis=0, concat_axis=0, tiled=True)  12.2 us
    all_to_all x1, blocking collectives, on_device(): lax.all_to_all(gram, OWNERS, split_axis=0, concat_axis=0, tiled=True)  11.6 us
    pallas_call x3, Pallas kernels, call(): pl.pallas_call(body, out_shape=out_shape, compiler_params=pltpu.CompilerP...  5.68 us
  transfers between devices with their start and end apart: 7, of which 4 were waited for; matrix products, arithmetic and copies ran while one was open for 1% of the time, Pallas kernels for 0%

profile of v3, /device:TPU:1, one launch (start us, length us, event | category | flops | bytes accessed | tf_op | source)
XLA Modules:
  0.0 95.5 jit_solution(2785364670935005554)
XLA Ops:
  0.7 0.0 copy-start
  0.7 1.5 %dynamic-slice_bitcast_fusion = (f32[80,896]{1,0:T(8,128)S(1)}, f32[80,896]{1,0:T(8,128)S(1)}, f32[80,896]{1,0:T(8,128)S(1)}, f32[80,896]{1,0:T(8,128)S(1)}, f32[80,896]{1,0:T(8,128)S(1)}) fusion(f32[1,80,7168]{2,1,0:T(8,128)} %param.2, s32[]{:T(128)S(6)} %select_n.31, s32[]{:T(128)S(6)} %select_n.29, s32[]{:T(128)S(6)} %select_n.27, s32[]{:T(128)S(6)} %select_n.25, ...), kind=kLoop, calls=%fused_computation.3 | loop fusion | bytes 2867220 | tf_op jit(solution)/shard_map/dynamic_slice | solution.py:121
  2.1 11.5 %collective-permute-start.5 = (f32[80,896]{1,0:T(8,128)S(1)}, f32[80,896]{1,0:T(8,128)S(1)}, u32[]{:S(2)}, u32[]{:S(2)}) collective-permute-start(f32[80,896]{1,0:T(8,128)S(1)} %get-tuple-element.11), channel_id=1, source_target_pairs={{0,64},{1,449},{64,0},{65,129},{128,192},{129,65},{192,128},{193,2... | collective-permute-start | bytes 860168 | tf_op jit(solution)/shard_map/ppermute | solution.py:131
  13.6 1.9 %collective-permute-start.3 = (f32[80,896]{1,0:T(8,128)S(1)}, f32[80,896]{1,0:T(8,128)S(1)}, u32[]{:S(2)}, u32[]{:S(2)}) collective-permute-start(f32[80,896]{1,0:T(8,128)S(1)} %get-tuple-element.12), channel_id=1, source_target_pairs={{0,64},{1,449},{64,0},{65,129},{128,192},{129,65},{192,128},{193,2... | collective-permute-start | bytes 860168 | tf_op jit(solution)/shard_map/ppermute | solution.py:131
  15.6 4.6 %collective-permute-start.1 = (f32[80,896]{1,0:T(8,128)S(1)}, f32[80,896]{1,0:T(8,128)S(1)}, u32[]{:S(2)}, u32[]{:S(2)}) collective-permute-start(f32[80,896]{1,0:T(8,128)S(1)} %get-tuple-element.13), channel_id=1, source_target_pairs={{0,64},{1,449},{64,0},{65,129},{128,192},{129,65},{192,128},{193,2... | collective-permute-start | bytes 860168 | tf_op jit(solution)/shard_map/ppermute | solution.py:131
  20.2 1.9 %collective-permute-start = (f32[80,896]{1,0:T(8,128)S(1)}, f32[80,896]{1,0:T(8,128)S(1)}, u32[]{:S(2)}, u32[]{:S(2)}) collective-permute-start(f32[80,896]{1,0:T(8,128)S(1)} %get-tuple-element.14), channel_id=1, source_target_pairs={{0,64},{1,449},{64,0},{65,129},{128,192},{129,65},{192,128},{193,2... | collective-permute-start | bytes 860168 | tf_op jit(solution)/shard_map/ppermute | solution.py:131
  22.1 0.0 collective-permute-done.5
  22.1 0.1 collective-permute-done.3
  22.2 3.1 %collective-permute-done.1 = f32[80,896]{1,0:T(8,128)S(1)} collective-permute-done((f32[80,896]{1,0:T(8,128)S(1)}, f32[80,896]{1,0:T(8,128)S(1)}, u32[]{:S(2)}, u32[]{:S(2)}) %collective-permute-start.1) | collective-permute-done | bytes 286752 | tf_op jit(solution)/shard_map/ppermute | solution.py:131
  25.3 1.2 %bitcast_add_fusion = (f32[80,896]{1,0:T(8,128)S(1)}, f32[80,896]{1,0:T(8,128)S(1)}, f32[80,896]{1,0:T(8,128)S(1)}) fusion(f32[80,896]{1,0:T(8,128)S(1)} %collective-permute-done.5, f32[1,80,7168]{2,1,0:T(8,128)} %param.2, s32[]{:T(128)S(6)} %select_n.30, f32[80,896]{1,0:T(8,128)S(1)} %collective-permute-done.3, s32[]{:T(128)S(6)} %select_n.28, ...), kind=kLoop, calls=%fused_computation | loop fusion | flops 215040 | bytes 2580492 | tf_op jit(solution)/shard_map/add | solution.py:134
  26.5 1.9 %collective-permute-start.6 = (f32[80,896]{1,0:T(8,128)S(1)}, f32[80,896]{1,0:T(8,128)S(1)}, u32[]{:S(2)}, u32[]{:S(2)}) collective-permute-start(f32[80,896]{1,0:T(8,128)S(1)} %get-tuple-element.8), channel_id=1, source_target_pairs={{0,448},{1,65},{64,128},{65,1},{128,64},{129,193},{192,256},{193,1... | collective-permute-start | bytes 860168 | tf_op jit(solution)/shard_map/ppermute | solution.py:131
  28.5 2.4 %collective-permute-start.4 = (f32[80,896]{1,0:T(8,128)S(1)}, f32[80,896]{1,0:T(8,128)S(1)}, u32[]{:S(2)}, u32[]{:S(2)}) collective-permute-start(f32[80,896]{1,0:T(8,128)S(1)} %get-tuple-element.9), channel_id=1, source_target_pairs={{0,384},{1,129},{64,192},{65,449},{128,0},{129,257},{192,320},{193... | collective-permute-start | bytes 860168 | tf_op jit(solution)/shard_map/ppermute | solution.py:131
  30.9 4.9 %collective-permute-start.2 = (f32[80,896]{1,0:T(8,128)S(1)}, f32[80,896]{1,0:T(8,128)S(1)}, u32[]{:S(2)}, u32[]{:S(2)}) collective-permute-start(f32[80,896]{1,0:T(8,128)S(1)} %get-tuple-element.10), channel_id=1, source_target_pairs={{0,320},{1,193},{64,256},{65,385},{128,448},{129,321},{192,384},{1... | collective-permute-start | bytes 860168 | tf_op jit(solution)/shard_map/ppermute | solution.py:131
  35.8 0.0 collective-permute-done.refs_1_
  35.9 0.0 collective-permute-done.6.refs_4_
  35.9 2.5 %collective-permute-done.4.refs_3_ = f32[80,896]{1,0:T(8,128)S(1)} collective-permute-done((f32[80,896]{1,0:T(8,128)S(1)}, f32[80,896]{1,0:T(8,128)S(1)}, u32[]{:S(2)}, u32[]{:S(2)}) %collective-permute-start.4) | collective-permute-done | bytes 286752 | tf_op jit(solution)/shard_map/ppermute | solution.py:131
  38.3 9.9 %collective-permute-done.2.refs_2_ = f32[80,896]{1,0:T(8,128)S(1)} collective-permute-done((f32[80,896]{1,0:T(8,128)S(1)}, f32[80,896]{1,0:T(8,128)S(1)}, u32[]{:S(2)}, u32[]{:S(2)}) %collective-permute-start.2) | collective-permute-done | bytes 286752 | tf_op jit(solution)/shard_map/ppermute | solution.py:131
  48.2 0.0 copy-done
  48.2 0.9 shard_map.41
  49.2 11.6 %all_to_all.15 = f32[8,72,128]{2,1,0:T(8,128)S(1)} all-to-all(f32[8,72,128]{2,1,0:T(8,128)S(1)} %get-tuple-element.6), channel_id=1, replica_groups=mesh['replica'=8,'y'=8,'x'=4,'core'=2] {'x','core'}, dimensions={0} | all-to-all | bytes 589824 | tf_op jit(solution)/shard_map/all_to_all | solution.py:149
  60.8 17.7 %all_to_all.16.parts_ref = f32[8,72,128]{2,1,0:T(8,128)S(1)} all-to-all(f32[8,72,128]{2,1,0:T(8,128)S(1)} %broadcast_in_dim.4), channel_id=1, replica_groups=mesh['replica'=8,'y'=8,'x'=4,'core'=2] {'y'}, dimensions={0} | all-to-all | bytes 589824 | tf_op jit(solution)/shard_map/all_to_all | solution.py:152
  78.5 3.4 %shard_map.42 = f32[72,128]{1,0:T(8,128)S(1)} custom-call(f32[8,72,128]{2,1,0:T(8,128)S(1)} %all_to_all.16.parts_ref), custom_call_target="tpu_custom_call" | custom-call | tf_op jit(solution)/shard_map/pallas_call | solution.py:104
  81.9 12.2 %all_to_all.17.product_ref = f32[8,72,128]{2,1,0:T(8,128)S(1)} all-to-all(f32[8,72,128]{2,1,0:T(8,128)S(1)} %broadcast_in_dim.5), channel_id=1, replica_groups=mesh['replica'=8,'y'=8,'x'=4,'core'=2] {'x','core'}, dimensions={0} | all-to-all | bytes 589824 | tf_op jit(solution)/shard_map/all_to_all | solution.py:155
  94.1 1.4 %shard_map.43 = f32[80,896]{1,0:T(8,128)} custom-call(f32[80,896]{1,0:T(8,128)S(1)} %get-tuple-element.5.blended_ref, f32[8,72,128]{2,1,0:T(8,128)S(1)} %all_to_all.17.product_ref), custom_call_target="tpu_custom_call" | custom-call | tf_op jit(solution)/shard_map/pallas_call | solution.py:104
  (3 shorter events, 0.1 us)
Async XLA Ops:
  0.7 47.6 %copy-start = (f32[80,896]{1,0:T(8,128)S(1)}, f32[80,896]{1,0:T(8,128)}, u32[]{:S(2)}) copy-start(f32[80,896]{1,0:T(8,128)} %refs_5_.1) | copy-start | bytes 860164
  2.1 20.0 %collective-permute-start.5 = (f32[80,896]{1,0:T(8,128)S(1)}, f32[80,896]{1,0:T(8,128)S(1)}, u32[]{:S(2)}, u32[]{:S(2)}) collective-permute-start(f32[80,896]{1,0:T(8,128)S(1)} %get-tuple-element.11), channel_id=1, source_target_pairs={{0,64},{1,449},{64,0},{65,129},{128,192},{129,65},{192,128},{193,2... | collective-permute-start | bytes 860168 | tf_op jit(solution)/shard_map/ppermute | solution.py:131
  13.6 8.6 %collective-permute-start.3 = (f32[80,896]{1,0:T(8,128)S(1)}, f32[80,896]{1,0:T(8,128)S(1)}, u32[]{:S(2)}, u32[]{:S(2)}) collective-permute-start(f32[80,896]{1,0:T(8,128)S(1)} %get-tuple-element.12), channel_id=1, source_target_pairs={{0,64},{1,449},{64,0},{65,129},{128,192},{129,65},{192,128},{193,2... | collective-permute-start | bytes 860168 | tf_op jit(solution)/shard_map/ppermute | solution.py:131
  15.6 9.7 %collective-permute-start.1 = (f32[80,896]{1,0:T(8,128)S(1)}, f32[80,896]{1,0:T(8,128)S(1)}, u32[]{:S(2)}, u32[]{:S(2)}) collective-permute-start(f32[80,896]{1,0:T(8,128)S(1)} %get-tuple-element.13), channel_id=1, source_target_pairs={{0,64},{1,449},{64,0},{65,129},{128,192},{129,65},{192,128},{193,2... | collective-permute-start | bytes 860168 | tf_op jit(solution)/shard_map/ppermute | solution.py:131
  20.2 15.7 %collective-permute-start = (f32[80,896]{1,0:T(8,128)S(1)}, f32[80,896]{1,0:T(8,128)S(1)}, u32[]{:S(2)}, u32[]{:S(2)}) collective-permute-start(f32[80,896]{1,0:T(8,128)S(1)} %get-tuple-element.14), channel_id=1, source_target_pairs={{0,64},{1,449},{64,0},{65,129},{128,192},{129,65},{192,128},{193,2... | collective-permute-start | bytes 860168 | tf_op jit(solution)/shard_map/ppermute | solution.py:131
  26.5 9.3 %collective-permute-start.6 = (f32[80,896]{1,0:T(8,128)S(1)}, f32[80,896]{1,0:T(8,128)S(1)}, u32[]{:S(2)}, u32[]{:S(2)}) collective-permute-start(f32[80,896]{1,0:T(8,128)S(1)} %get-tuple-element.8), channel_id=1, source_target_pairs={{0,448},{1,65},{64,128},{65,1},{128,64},{129,193},{192,256},{193,1... | collective-permute-start | bytes 860168 | tf_op jit(solution)/shard_map/ppermute | solution.py:131
  28.5 9.9 %collective-permute-start.4 = (f32[80,896]{1,0:T(8,128)S(1)}, f32[80,896]{1,0:T(8,128)S(1)}, u32[]{:S(2)}, u32[]{:S(2)}) collective-permute-start(f32[80,896]{1,0:T(8,128)S(1)} %get-tuple-element.9), channel_id=1, source_target_pairs={{0,384},{1,129},{64,192},{65,449},{128,0},{129,257},{192,320},{193... | collective-permute-start | bytes 860168 | tf_op jit(solution)/shard_map/ppermute | solution.py:131
  30.9 17.3 %collective-permute-start.2 = (f32[80,896]{1,0:T(8,128)S(1)}, f32[80,896]{1,0:T(8,128)S(1)}, u32[]{:S(2)}, u32[]{:S(2)}) collective-permute-start(f32[80,896]{1,0:T(8,128)S(1)} %get-tuple-element.10), channel_id=1, source_target_pairs={{0,320},{1,193},{64,256},{65,385},{128,448},{129,321},{192,384},{1... | collective-permute-start | bytes 860168 | tf_op jit(solution)/shard_map/ppermute | solution.py:131

commit v4 on v3

--- a/solution.py
+++ b/solution.py
@@ -130,9 +130,14 @@
                 pairs.append((2 * i + c, 2 * j + c))
         return lax.ppermute(value, ("replica", "core"), pairs)
 
-    partner = [send(chunk(k), 1) for k in (4, 3, 2, 1)]
-    others = [send(chunk(-k) + part, -k) for k, part in zip((3, 2, 1), partner)]
-    return chunk(0), partner[3], *others
+    offsets = (4, 3, 2, 1, -3, -2, -1, 0)
+    chunks = dict(zip(offsets, lax.optimization_barrier(tuple(chunk(k) for k in offsets))))
+    fourth, third, second = (send(chunks[k], 1) for k in (4, 3, 2))
+    relayed = send(chunks[-3] + fourth, -2)
+    partner = send(chunks[1], 1)
+    from_second = send(chunks[-2] + third, -2)
+    from_first = send(chunks[-1] + second + relayed, -1)
+    return chunks[0], partner, from_second, from_first
 
 
 def on_device(grad_partials, momentum):

time: 96.3 us -> 92.8 us (0.964)
  waiting for transfers between devices: 15.5 us -> 13.4 us
  other arithmetic: 1.25 us -> 0.14 us
    ppermute x7, waiting for transfers between devices: 15.5 us -> 13.4 us  [send(): return lax.ppermute(value, ('replica', 'core'), pairs)]
    add x1 -> x3, other arithmetic: 1.23 us -> 0.12 us  [the longest x1 0.05 us: replica_sums(): from_first = send(chunks[-1] + second + relayed, -1)]
  transfers between devices with their start and end apart: 7 -> 7, of which waited for: 4 -> 3; matrix products, arithmetic and copies ran while one was open for 1% -> 0% of each run, Pallas kernels for 0% -> 0%
where the time goes in v4:
time: 92.8 us; the launch traced here: 92.4 us
  blocking collectives  42.3 us (46%)
  starting transfers between devices  28.3 us (30%)
  waiting for transfers between devices  13.4 us (14%)
  Pallas kernels  5.66 us (6%)
  local copies, waits for them, and re-layouts  1.79 us (2%)
    ppermute x7, starting transfers between devices, send(): return lax.ppermute(value, ('replica', 'core'), pairs)  28.3 us
    all_to_all x1, blocking collectives, on_device(): parts = lax.all_to_all(parts, 'y', split_axis=0, concat_axis=0, tiled=True)  17.7 us
    ppermute x7, waiting for transfers between devices, send(): return lax.ppermute(value, ('replica', 'core'), pairs)  13.4 us
    all_to_all x1, blocking collectives, on_device(): lax.all_to_all(gram, OWNERS, split_axis=0, concat_axis=0, tiled=True)  12.5 us
    all_to_all x1, blocking collectives, on_device(): lax.all_to_all(products, OWNERS, split_axis=0, concat_axis=0, tiled=True)  12.2 us
    pallas_call x3, Pallas kernels, call(): pl.pallas_call(body, out_shape=out_shape, compiler_params=pltpu.CompilerP...  5.66 us
  transfers between devices with their start and end apart: 7, of which 3 were waited for; matrix products, arithmetic and copies ran while one was open for 0% of the time, Pallas kernels for 0%

profile of v4, /device:TPU:1, one launch (start us, length us, event | category | flops | bytes accessed | tf_op | source)
XLA Modules:
  0.0 92.4 jit_solution(16785205458126074441)
XLA Ops:
  0.7 1.7 %dynamic-slice_bitcast_fusion = (f32[80,896]{1,0:T(8,128)S(1)}, f32[80,896]{1,0:T(8,128)S(1)}, f32[80,896]{1,0:T(8,128)S(1)}, f32[80,896]{1,0:T(8,128)S(1)}, f32...) fusion(f32[1,80,7168]{2,1,0:T(8,128)} %param.2, s32[]{:T(128)S(6)} %select_n.31, ...), kind=kLoop, calls=%fused_computation.1 | loop fusion | bytes 4587552 | tf_op jit(solution)/shard_map/dynamic_slice | solution.py:121
  2.4 0.0 copy-start
  2.5 11.6 %collective-permute-start.4 = (f32[80,896]{1,0:T(8,128)S(1)}, f32[80,896]{1,0:T(8,128)S(1)}, u32[]{:S(2)}, u32[]{:S(2)}) collective-permute-start(f32[80,896]{1,0:T(8,128)S(1)} %get-tuple-element.20), channel_id=1, source_target_pairs={{0,64},{1,449},{64,0},{65,129},{128,192},{129,65},{192,128},{193,2... | collective-permute-start | bytes 860168 | tf_op jit(solution)/shard_map/ppermute | solution.py:131
  14.1 1.9 %collective-permute-start.1 = (f32[80,896]{1,0:T(8,128)S(1)}, f32[80,896]{1,0:T(8,128)S(1)}, u32[]{:S(2)}, u32[]{:S(2)}) collective-permute-start(f32[80,896]{1,0:T(8,128)S(1)} %get-tuple-element.16), channel_id=1, source_target_pairs={{0,64},{1,449},{64,0},{65,129},{128,192},{129,65},{192,128},{193,2... | collective-permute-start | bytes 860168 | tf_op jit(solution)/shard_map/ppermute | solution.py:131
  16.0 4.6 %collective-permute-start.3 = (f32[80,896]{1,0:T(8,128)S(1)}, f32[80,896]{1,0:T(8,128)S(1)}, u32[]{:S(2)}, u32[]{:S(2)}) collective-permute-start(f32[80,896]{1,0:T(8,128)S(1)} %get-tuple-element.18), channel_id=1, source_target_pairs={{0,64},{1,449},{64,0},{65,129},{128,192},{129,65},{192,128},{193,2... | collective-permute-start | bytes 860168 | tf_op jit(solution)/shard_map/ppermute | solution.py:131
  20.6 0.0 collective-permute-done.4
  20.7 1.9 %collective-permute-start.5 = (f32[80,896]{1,0:T(8,128)S(1)}, f32[80,896]{1,0:T(8,128)S(1)}, u32[]{:S(2)}, u32[]{:S(2)}) collective-permute-start(f32[80,896]{1,0:T(8,128)S(1)} %add.110), channel_id=1, source_target_pairs={{0,384},{1,129},{64,192},{65,449},{128,0},{129,257},{192,320},{193... | collective-permute-start | bytes 860168 | tf_op jit(solution)/shard_map/ppermute | solution.py:131
  22.6 2.1 %collective-permute-start = (f32[80,896]{1,0:T(8,128)S(1)}, f32[80,896]{1,0:T(8,128)S(1)}, u32[]{:S(2)}, u32[]{:S(2)}) collective-permute-start(f32[80,896]{1,0:T(8,128)S(1)} %get-tuple-element.14), channel_id=1, source_target_pairs={{0,64},{1,449},{64,0},{65,129},{128,192},{129,65},{192,128},{193,2... | collective-permute-start | bytes 860168 | tf_op jit(solution)/shard_map/ppermute | solution.py:131
  24.7 0.0 collective-permute-done.1
  24.8 4.2 %collective-permute-start.2 = (f32[80,896]{1,0:T(8,128)S(1)}, f32[80,896]{1,0:T(8,128)S(1)}, u32[]{:S(2)}, u32[]{:S(2)}) collective-permute-start(f32[80,896]{1,0:T(8,128)S(1)} %add.108), channel_id=1, source_target_pairs={{0,384},{1,129},{64,192},{65,449},{128,0},{129,257},{192,320},{193... | collective-permute-start | bytes 860168 | tf_op jit(solution)/shard_map/ppermute | solution.py:131
  29.0 0.0 collective-permute-done.3
  29.0 7.6 %collective-permute-done.5 = f32[80,896]{1,0:T(8,128)S(1)} collective-permute-done((f32[80,896]{1,0:T(8,128)S(1)}, f32[80,896]{1,0:T(8,128)S(1)}, u32[]{:S(2)}, u32[]{:S(2)}) %collective-permute-start.5) | collective-permute-done | bytes 286752 | tf_op jit(solution)/shard_map/ppermute | solution.py:131
  36.6 1.9 %collective-permute-start.6 = (f32[80,896]{1,0:T(8,128)S(1)}, f32[80,896]{1,0:T(8,128)S(1)}, u32[]{:S(2)}, u32[]{:S(2)}) collective-permute-start(f32[80,896]{1,0:T(8,128)S(1)} %add_add_fusion), channel_id=1, source_target_pairs={{0,448},{1,65},{64,128},{65,1},{128,64},{129,193},{192,256},{193,1... | collective-permute-start | bytes 860168 | tf_op jit(solution)/shard_map/ppermute | solution.py:131
  38.6 0.0 collective-permute-done.refs_1_
  38.6 3.8 %collective-permute-done.2.refs_2_ = f32[80,896]{1,0:T(8,128)S(1)} collective-permute-done((f32[80,896]{1,0:T(8,128)S(1)}, f32[80,896]{1,0:T(8,128)S(1)}, u32[]{:S(2)}, u32[]{:S(2)}) %collective-permute-start.2) | collective-permute-done | bytes 286752 | tf_op jit(solution)/shard_map/ppermute | solution.py:131
  42.4 1.9 %collective-permute-done.6.refs_3_ = f32[80,896]{1,0:T(8,128)S(1)} collective-permute-done((f32[80,896]{1,0:T(8,128)S(1)}, f32[80,896]{1,0:T(8,128)S(1)}, u32[]{:S(2)}, u32[]{:S(2)}) %collective-permute-start.6) | collective-permute-done | bytes 286752 | tf_op jit(solution)/shard_map/ppermute | solution.py:131
  44.3 0.0 copy-done
  44.3 0.9 shard_map.41
  45.2 12.5 %all_to_all.15 = f32[8,72,128]{2,1,0:T(8,128)S(1)} all-to-all(f32[8,72,128]{2,1,0:T(8,128)S(1)} %get-tuple-element.22), channel_id=1, replica_groups=mesh['replica'=8,'y'=8,'x'=4,'core'=2] {'x','core'}, dimensions={0} | all-to-all | bytes 589824 | tf_op jit(solution)/shard_map/all_to_all | solution.py:154
  57.8 17.7 %all_to_all.16.parts_ref = f32[8,72,128]{2,1,0:T(8,128)S(1)} all-to-all(f32[8,72,128]{2,1,0:T(8,128)S(1)} %broadcast_in_dim.4), channel_id=1, replica_groups=mesh['replica'=8,'y'=8,'x'=4,'core'=2] {'y'}, dimensions={0} | all-to-all | bytes 589824 | tf_op jit(solution)/shard_map/all_to_all | solution.py:157
  75.5 3.4 %shard_map.42 = f32[72,128]{1,0:T(8,128)S(1)} custom-call(f32[8,72,128]{2,1,0:T(8,128)S(1)} %all_to_all.16.parts_ref), custom_call_target="tpu_custom_call" | custom-call | tf_op jit(solution)/shard_map/pallas_call | solution.py:104
  78.9 12.2 %all_to_all.17.product_ref = f32[8,72,128]{2,1,0:T(8,128)S(1)} all-to-all(f32[8,72,128]{2,1,0:T(8,128)S(1)} %broadcast_in_dim.5), channel_id=1, replica_groups=mesh['replica'=8,'y'=8,'x'=4,'core'=2] {'x','core'}, dimensions={0} | all-to-all | bytes 589824 | tf_op jit(solution)/shard_map/all_to_all | solution.py:160
  91.0 1.4 %shard_map.43 = f32[80,896]{1,0:T(8,128)} custom-call(f32[80,896]{1,0:T(8,128)S(1)} %get-tuple-element.21.blended_ref, f32[8,72,128]{2,1,0:T(8,128)S(1)} %all_to_all.17.product_ref), custom_call_target="tpu_custom_call" | custom-call | tf_op jit(solution)/shard_map/pallas_call | solution.py:104
  (6 shorter events, 0.2 us)
Async XLA Ops:
  2.4 41.9 %copy-start = (f32[80,896]{1,0:T(8,128)S(1)}, f32[80,896]{1,0:T(8,128)}, u32[]{:S(2)}) copy-start(f32[80,896]{1,0:T(8,128)} %refs_4_.1) | copy-start | bytes 860164
  2.5 18.1 %collective-permute-start.4 = (f32[80,896]{1,0:T(8,128)S(1)}, f32[80,896]{1,0:T(8,128)S(1)}, u32[]{:S(2)}, u32[]{:S(2)}) collective-permute-start(f32[80,896]{1,0:T(8,128)S(1)} %get-tuple-element.20), channel_id=1, source_target_pairs={{0,64},{1,449},{64,0},{65,129},{128,192},{129,65},{192,128},{193,2... | collective-permute-start | bytes 860168 | tf_op jit(solution)/shard_map/ppermute | solution.py:131
  14.1 10.6 %collective-permute-start.1 = (f32[80,896]{1,0:T(8,128)S(1)}, f32[80,896]{1,0:T(8,128)S(1)}, u32[]{:S(2)}, u32[]{:S(2)}) collective-permute-start(f32[80,896]{1,0:T(8,128)S(1)} %get-tuple-element.16), channel_id=1, source_target_pairs={{0,64},{1,449},{64,0},{65,129},{128,192},{129,65},{192,128},{193,2... | collective-permute-start | bytes 860168 | tf_op jit(solution)/shard_map/ppermute | solution.py:131
  16.0 13.0 %collective-permute-start.3 = (f32[80,896]{1,0:T(8,128)S(1)}, f32[80,896]{1,0:T(8,128)S(1)}, u32[]{:S(2)}, u32[]{:S(2)}) collective-permute-start(f32[80,896]{1,0:T(8,128)S(1)} %get-tuple-element.18), channel_id=1, source_target_pairs={{0,64},{1,449},{64,0},{65,129},{128,192},{129,65},{192,128},{193,2... | collective-permute-start | bytes 860168 | tf_op jit(solution)/shard_map/ppermute | solution.py:131
  20.7 15.9 %collective-permute-start.5 = (f32[80,896]{1,0:T(8,128)S(1)}, f32[80,896]{1,0:T(8,128)S(1)}, u32[]{:S(2)}, u32[]{:S(2)}) collective-permute-start(f32[80,896]{1,0:T(8,128)S(1)} %add.110), channel_id=1, source_target_pairs={{0,384},{1,129},{64,192},{65,449},{128,0},{129,257},{192,320},{193... | collective-permute-start | bytes 860168 | tf_op jit(solution)/shard_map/ppermute | solution.py:131
  22.6 16.0 %collective-permute-start = (f32[80,896]{1,0:T(8,128)S(1)}, f32[80,896]{1,0:T(8,128)S(1)}, u32[]{:S(2)}, u32[]{:S(2)}) collective-permute-start(f32[80,896]{1,0:T(8,128)S(1)} %get-tuple-element.14), channel_id=1, source_target_pairs={{0,64},{1,449},{64,0},{65,129},{128,192},{129,65},{192,128},{193,2... | collective-permute-start | bytes 860168 | tf_op jit(solution)/shard_map/ppermute | solution.py:131
  24.8 17.6 %collective-permute-start.2 = (f32[80,896]{1,0:T(8,128)S(1)}, f32[80,896]{1,0:T(8,128)S(1)}, u32[]{:S(2)}, u32[]{:S(2)}) collective-permute-start(f32[80,896]{1,0:T(8,128)S(1)} %add.108), channel_id=1, source_target_pairs={{0,384},{1,129},{64,192},{65,449},{128,0},{129,257},{192,320},{193... | collective-permute-start | bytes 860168 | tf_op jit(solution)/shard_map/ppermute | solution.py:131
  36.6 7.7 %collective-permute-start.6 = (f32[80,896]{1,0:T(8,128)S(1)}, f32[80,896]{1,0:T(8,128)S(1)}, u32[]{:S(2)}, u32[]{:S(2)}) collective-permute-start(f32[80,896]{1,0:T(8,128)S(1)} %add_add_fusion), channel_id=1, source_target_pairs={{0,448},{1,65},{64,128},{65,1},{128,64},{129,193},{192,256},{193,1... | collective-permute-start | bytes 860168 | tf_op jit(solution)/shard_map/ppermute | solution.py:131

commit v5 on v4

--- a/solution.py
+++ b/solution.py
@@ -13,6 +13,7 @@
 HALF = HEAD_DIM // 2
 PACKED = HALF + 8
 ITERS = 5
+VMEM = 32 * 1024 * 1024
 
 quintic_a = 3.4445
 quintic_b = -4.775
@@ -65,17 +66,21 @@
     blended = grad_sum + beta_decay * momentum_next
     blended_ref[...] = blended
     heads = blended.shape[1] // HEAD_DIM
-    for h in range(gram_ref.shape[0]):
+    cores = gram_ref.shape[0]
+    for h in range(cores * gram_ref.shape[1]):
+        core, x = h % cores, h // cores
         if h < heads:
             part = blended[:, h * HEAD_DIM : (h + 1) * HEAD_DIM]
             body, diagonal = pack(dot(part, part, ((0,), (0,))))
-            gram_ref[h, :HALF] = body
-            gram_ref[h, HALF:] = diagonal
+            gram_ref[core, x, :HALF] = body
+            gram_ref[core, x, HALF:] = diagonal
         else:
-            gram_ref[h] = jnp.zeros_like(gram_ref[h])
-
-
-def newton_schulz(parts_ref, out_ref):
+            gram_ref[core, x] = jnp.zeros_like(gram_ref[core, x])
+
+
+def newton_schulz(parts_ref, next_ref, out_ref, next_out_ref, sem):
+    write = pltpu.make_async_copy(next_ref, next_out_ref, sem)
+    write.start()
     packed = jnp.sum(parts_ref[...], axis=0)
     total = jnp.sum(packed[HALF : HALF + 1])
     scale = 1.0 / (jnp.sqrt(total) + norm_eps)
@@ -92,19 +97,25 @@
     body, diagonal = pack(product * (factor * scale))
     out_ref[:HALF] = body
     out_ref[HALF:] = diagonal
-
-
-def apply(blended_ref, product_ref, out_ref):
+    write.wait()
+
+
+def apply(blended_ref, product_ref, out_ref, held, sems):
+    writes = []
     for h in range(out_ref.shape[1] // HEAD_DIM):
         cols = slice(h * HEAD_DIM, (h + 1) * HEAD_DIM)
-        out_ref[:, cols] = dot(blended_ref[:, cols], unpack(product_ref[h]))
+        held[:, cols] = dot(blended_ref[:, cols], unpack(product_ref[h]))
+        writes.append(pltpu.make_async_copy(held.at[:, cols], out_ref.at[:, cols], sems.at[h]))
+        writes[-1].start()
+    for write in writes:
+        write.wait()
 
 
 def call(body, out_shape, *args):
     return pl.pallas_call(
         body,
         out_shape=out_shape,
-        compiler_params=pltpu.CompilerParams(vmem_limit_bytes=32 * 1024 * 1024),
+        compiler_params=pltpu.CompilerParams(vmem_limit_bytes=VMEM),
     )(*args)
 
 
@@ -145,20 +156,37 @@
     cols, rows = momentum.shape
     heads = rows // HEAD_DIM
     owners = lax.axis_size(OWNERS)
+    owner_grid = (lax.axis_size("core"), lax.axis_size("x"))
     momentum_next, blended, gram = call(
         momentum_and_gram,
-        (f32(cols, rows), f32(cols, rows), f32(owners, PACKED, HEAD_DIM)),
+        (f32(cols, rows), f32(cols, rows), f32(*owner_grid, PACKED, HEAD_DIM)),
         *terms,
         momentum,
     )
-    parts = lax.all_to_all(gram, OWNERS, split_axis=0, concat_axis=0, tiled=True)
+    both = lax.all_gather(gram, "core")
+    mine = lax.dynamic_index_in_dim(both, lax.axis_index("core"), axis=1, keepdims=False)
+    parts = lax.all_to_all(jnp.sum(mine, axis=0), "x", split_axis=0, concat_axis=0, tiled=True)
     part = jnp.sum(parts, axis=0)
     parts = jnp.broadcast_to(part[None], (lax.axis_size("y"), PACKED, HEAD_DIM))
     parts = lax.all_to_all(parts, "y", split_axis=0, concat_axis=0, tiled=True)
-    product = call(newton_schulz, f32(PACKED, HEAD_DIM), parts)
+    product, momentum_next = pl.pallas_call(
+        newton_schulz,
+        in_specs=[pl.BlockSpec(memory_space=pltpu.VMEM), pl.BlockSpec(memory_space=pl.ANY)],
+        out_specs=[pl.BlockSpec(memory_space=pltpu.VMEM), pl.BlockSpec(memory_space=pl.ANY)],
+        out_shape=[f32(PACKED, HEAD_DIM), f32(cols, rows)],
+        scratch_shapes=[pltpu.SemaphoreType.DMA],
+        compiler_params=pltpu.CompilerParams(vmem_limit_bytes=VMEM),
+    )(parts, momentum_next)
     products = jnp.broadcast_to(product[None], (owners, PACKED, HEAD_DIM))
     products = lax.all_to_all(products, OWNERS, split_axis=0, concat_axis=0, tiled=True)
-    update = call(apply, f32(cols, rows), blended, products)
+    update = pl.pallas_call(
+        apply,
+        in_specs=[pl.BlockSpec(memory_space=pltpu.VMEM)] * 2,
+        out_specs=pl.BlockSpec(memory_space=pl.ANY),
+        out_shape=f32(cols, rows),
+        scratch_shapes=[pltpu.VMEM((cols, rows), jnp.float32), pltpu.SemaphoreType.DMA((heads,))],
+        compiler_params=pltpu.CompilerParams(vmem_limit_bytes=VMEM),
+    )(blended, products)
     return update, momentum_next
 
 

time: 92.8 us -> 91.9 us (level)
    pallas_call x3 -> x1, Pallas kernels: 5.66 us -> 0.69 us  [call(): pl.pallas_call(body, out_shape=out_shape, compiler_params=pltpu.CompilerP...]
    pallas_call x0 -> x2, Pallas kernels: none -> 4.74 us  [the longest x1 3.38 us: on_device(): pl.pallas_call(newton_schulz, in_specs=[pl.BlockSpec(memory_space=pltpu.V...]
    all_to_all x1, blocking collectives: 12.5 us -> 8.1 us  [on_device(): lax.all_to_all(jnp.sum(mine, axis=0), 'x', split_axis=0, concat_axis=0, t...]
    all_gather x0 -> x1, blocking collectives: none -> 3.53 us  [on_device(): both = lax.all_gather(gram, 'core')]
    all_to_all x1, blocking collectives: 12.2 us -> 14 us  [on_device(): lax.all_to_all(products, OWNERS, split_axis=0, concat_axis=0, tiled=True)]
    all_to_all x1, blocking collectives: 17.7 us -> 16 us  [on_device(): parts = lax.all_to_all(parts, 'y', split_axis=0, concat_axis=0, tiled=True)]
where the time goes in v5:
time: 91.9 us; the launch traced here: 91.5 us
  blocking collectives  41.6 us (45%)
  starting transfers between devices  28.3 us (31%)
  waiting for transfers between devices  13.4 us (15%)
  Pallas kernels  5.43 us (6%)
  local copies, waits for them, and re-layouts  1.79 us (2%)
    ppermute x7, starting transfers between devices, send(): return lax.ppermute(value, ('replica', 'core'), pairs)  28.3 us
    all_to_all x1, blocking collectives, on_device(): parts = lax.all_to_all(parts, 'y', split_axis=0, concat_axis=0, tiled=True)  16 us
    all_to_all x1, blocking collectives, on_device(): lax.all_to_all(products, OWNERS, split_axis=0, concat_axis=0, tiled=True)  14 us
    ppermute x7, waiting for transfers between devices, send(): return lax.ppermute(value, ('replica', 'core'), pairs)  13.4 us
    all_to_all x1, blocking collectives, on_device(): lax.all_to_all(jnp.sum(mine, axis=0), 'x', split_axis=0, concat_axis=0, t...  8.1 us
    all_gather x1, blocking collectives, on_device(): both = lax.all_gather(gram, 'core')  3.53 us
    pallas_call x1, Pallas kernels, on_device(): pl.pallas_call(newton_schulz, in_specs=[pl.BlockSpec(memory_space=pltpu.V...  3.38 us
  transfers between devices with their start and end apart: 7, of which 3 were waited for; matrix products, arithmetic and copies ran while one was open for 0% of the time, Pallas kernels for 0%

profile of v5, /device:TPU:1, one launch (start us, length us, event | category | flops | bytes accessed | tf_op | source)
XLA Modules:
  0.0 91.5 jit_solution(9547964357219308048)
XLA Ops:
  0.7 1.7 %dynamic-slice_bitcast_fusion = (f32[80,896]{1,0:T(8,128)S(1)}, f32[80,896]{1,0:T(8,128)S(1)}, f32[80,896]{1,0:T(8,128)S(1)}, f32[80,896]{1,0:T(8,128)S(1)}, f32...) fusion(f32[1,80,7168]{2,1,0:T(8,128)} %param.2, s32[]{:T(128)S(6)} %select_n.35, ...), kind=kLoop, calls=%fused_computation.2 | loop fusion | bytes 4587552 | tf_op jit(solution)/shard_map/dynamic_slice | solution.py:132
  2.4 0.0 copy-start
  2.5 11.6 %collective-permute-start.4 = (f32[80,896]{1,0:T(8,128)S(1)}, f32[80,896]{1,0:T(8,128)S(1)}, u32[]{:S(2)}, u32[]{:S(2)}) collective-permute-start(f32[80,896]{1,0:T(8,128)S(1)} %get-tuple-element.22), channel_id=1, source_target_pairs={{0,64},{1,449},{64,0},{65,129},{128,192},{129,65},{192,128},{193,2... | collective-permute-start | bytes 860168 | tf_op jit(solution)/shard_map/ppermute | solution.py:142
  14.1 1.9 %collective-permute-start.1 = (f32[80,896]{1,0:T(8,128)S(1)}, f32[80,896]{1,0:T(8,128)S(1)}, u32[]{:S(2)}, u32[]{:S(2)}) collective-permute-start(f32[80,896]{1,0:T(8,128)S(1)} %get-tuple-element.18), channel_id=1, source_target_pairs={{0,64},{1,449},{64,0},{65,129},{128,192},{129,65},{192,128},{193,2... | collective-permute-start | bytes 860168 | tf_op jit(solution)/shard_map/ppermute | solution.py:142
  16.0 4.6 %collective-permute-start.3 = (f32[80,896]{1,0:T(8,128)S(1)}, f32[80,896]{1,0:T(8,128)S(1)}, u32[]{:S(2)}, u32[]{:S(2)}) collective-permute-start(f32[80,896]{1,0:T(8,128)S(1)} %get-tuple-element.20), channel_id=1, source_target_pairs={{0,64},{1,449},{64,0},{65,129},{128,192},{129,65},{192,128},{193,2... | collective-permute-start | bytes 860168 | tf_op jit(solution)/shard_map/ppermute | solution.py:142
  20.6 0.0 collective-permute-done.4
  20.7 1.9 %collective-permute-start.5 = (f32[80,896]{1,0:T(8,128)S(1)}, f32[80,896]{1,0:T(8,128)S(1)}, u32[]{:S(2)}, u32[]{:S(2)}) collective-permute-start(f32[80,896]{1,0:T(8,128)S(1)} %add.114), channel_id=1, source_target_pairs={{0,384},{1,129},{64,192},{65,449},{128,0},{129,257},{192,320},{193... | collective-permute-start | bytes 860168 | tf_op jit(solution)/shard_map/ppermute | solution.py:142
  22.6 2.1 %collective-permute-start = (f32[80,896]{1,0:T(8,128)S(1)}, f32[80,896]{1,0:T(8,128)S(1)}, u32[]{:S(2)}, u32[]{:S(2)}) collective-permute-start(f32[80,896]{1,0:T(8,128)S(1)} %get-tuple-element.16), channel_id=1, source_target_pairs={{0,64},{1,449},{64,0},{65,129},{128,192},{129,65},{192,128},{193,2... | collective-permute-start | bytes 860168 | tf_op jit(solution)/shard_map/ppermute | solution.py:142
  24.7 0.0 collective-permute-done.1
  24.8 4.2 %collective-permute-start.2 = (f32[80,896]{1,0:T(8,128)S(1)}, f32[80,896]{1,0:T(8,128)S(1)}, u32[]{:S(2)}, u32[]{:S(2)}) collective-permute-start(f32[80,896]{1,0:T(8,128)S(1)} %add.112), channel_id=1, source_target_pairs={{0,384},{1,129},{64,192},{65,449},{128,0},{129,257},{192,320},{193... | collective-permute-start | bytes 860168 | tf_op jit(solution)/shard_map/ppermute | solution.py:142
  29.0 0.0 collective-permute-done.3
  29.0 7.6 %collective-permute-done.5 = f32[80,896]{1,0:T(8,128)S(1)} collective-permute-done((f32[80,896]{1,0:T(8,128)S(1)}, f32[80,896]{1,0:T(8,128)S(1)}, u32[]{:S(2)}, u32[]{:S(2)}) %collective-permute-start.5) | collective-permute-done | bytes 286752 | tf_op jit(solution)/shard_map/ppermute | solution.py:142
  36.6 0.1 add_add_fusion
  36.7 1.9 %collective-permute-start.6 = (f32[80,896]{1,0:T(8,128)S(1)}, f32[80,896]{1,0:T(8,128)S(1)}, u32[]{:S(2)}, u32[]{:S(2)}) collective-permute-start(f32[80,896]{1,0:T(8,128)S(1)} %add_add_fusion), channel_id=1, source_target_pairs={{0,448},{1,65},{64,128},{65,1},{128,64},{129,193},{192,256},{193,1... | collective-permute-start | bytes 860168 | tf_op jit(solution)/shard_map/ppermute | solution.py:142
  38.6 0.0 collective-permute-done.refs_1_
  38.6 3.8 %collective-permute-done.2.refs_2_ = f32[80,896]{1,0:T(8,128)S(1)} collective-permute-done((f32[80,896]{1,0:T(8,128)S(1)}, f32[80,896]{1,0:T(8,128)S(1)}, u32[]{:S(2)}, u32[]{:S(2)}) %collective-permute-start.2) | collective-permute-done | bytes 286752 | tf_op jit(solution)/shard_map/ppermute | solution.py:142
  42.4 1.9 %collective-permute-done.6.refs_3_ = f32[80,896]{1,0:T(8,128)S(1)} collective-permute-done((f32[80,896]{1,0:T(8,128)S(1)}, f32[80,896]{1,0:T(8,128)S(1)}, u32[]{:S(2)}, u32[]{:S(2)}) %collective-permute-start.6) | collective-permute-done | bytes 286752 | tf_op jit(solution)/shard_map/ppermute | solution.py:142
  44.3 0.7 shard_map.41
  45.0 3.5 %all-gather = f32[4,4,72,128]{3,2,1,0:T(8,128)S(1)} all-gather(f32[2,4,72,128]{3,2,1,0:T(8,128)S(1)} %get-tuple-element.24), channel_id=2, replica_groups=mesh['replica'=8,'y'=8,'x'=4,'core'=2] {'core'}, dimensions={0}, use_global_device_ids=true | all-gather | bytes 884736 | tf_op jit(solution)/shard_map/all_gather | solution.py:166
  48.6 8.1 %all_to_all.15 = f32[4,72,128]{2,1,0:T(8,128)S(1)} all-to-all(f32[4,72,128]{2,1,0:T(8,128)S(1)} %dynamic-slice_reduce_fusion), channel_id=1, replica_groups=mesh['replica'=8,'y'=8,'x'=4,'core'=2] {'x'}, dimensions={0} | all-to-all | bytes 294912 | tf_op jit(solution)/shard_map/all_to_all | solution.py:168
  56.7 16.0 %all_to_all.16.parts_ref = f32[8,72,128]{2,1,0:T(8,128)S(1)} all-to-all(f32[8,72,128]{2,1,0:T(8,128)S(1)} %broadcast_in_dim.4), channel_id=1, replica_groups=mesh['replica'=8,'y'=8,'x'=4,'core'=2] {'y'}, dimensions={0} | all-to-all | bytes 589824 | tf_op jit(solution)/shard_map/all_to_all | solution.py:171
  72.7 3.4 %shard_map.42 = (f32[72,128]{1,0:T(8,128)S(1)}, f32[80,896]{1,0:T(8,128)}) custom-call(f32[8,72,128]{2,1,0:T(8,128)S(1)} %all_to_all.16.parts_ref, f32[80,896]{1,0:T(8,128)S(1)} %get-tuple-element.25.next_ref), custom_call_target="tpu_custom_call" | custom-call | tf_op jit(solution)/shard_map/pallas_call | solution.py:172
  76.1 14.0 %all_to_all.17.product_ref = f32[8,72,128]{2,1,0:T(8,128)S(1)} all-to-all(f32[8,72,128]{2,1,0:T(8,128)S(1)} %broadcast_in_dim.5), channel_id=1, replica_groups=mesh['replica'=8,'y'=8,'x'=4,'core'=2] {'x','core'}, dimensions={0} | all-to-all | bytes 589824 | tf_op jit(solution)/shard_map/all_to_all | solution.py:181
  90.1 1.4 %shard_map.43 = f32[80,896]{1,0:T(8,128)} custom-call(f32[80,896]{1,0:T(8,128)S(1)} %get-tuple-element.23.blended_ref, f32[8,72,128]{2,1,0:T(8,128)S(1)} %all_to_all.17.product_ref), custom_call_target="tpu_custom_call" | custom-call | tf_op jit(solution)/shard_map/pallas_call | solution.py:182
  (7 shorter events, 0.1 us)
Async XLA Ops:
  2.4 41.9 %copy-start = (f32[80,896]{1,0:T(8,128)S(1)}, f32[80,896]{1,0:T(8,128)}, u32[]{:S(2)}) copy-start(f32[80,896]{1,0:T(8,128)} %refs_4_.1) | copy-start | bytes 860164
  2.5 18.1 %collective-permute-start.4 = (f32[80,896]{1,0:T(8,128)S(1)}, f32[80,896]{1,0:T(8,128)S(1)}, u32[]{:S(2)}, u32[]{:S(2)}) collective-permute-start(f32[80,896]{1,0:T(8,128)S(1)} %get-tuple-element.22), channel_id=1, source_target_pairs={{0,64},{1,449},{64,0},{65,129},{128,192},{129,65},{192,128},{193,2... | collective-permute-start | bytes 860168 | tf_op jit(solution)/shard_map/ppermute | solution.py:142
  14.1 10.6 %collective-permute-start.1 = (f32[80,896]{1,0:T(8,128)S(1)}, f32[80,896]{1,0:T(8,128)S(1)}, u32[]{:S(2)}, u32[]{:S(2)}) collective-permute-start(f32[80,896]{1,0:T(8,128)S(1)} %get-tuple-element.18), channel_id=1, source_target_pairs={{0,64},{1,449},{64,0},{65,129},{128,192},{129,65},{192,128},{193,2... | collective-permute-start | bytes 860168 | tf_op jit(solution)/shard_map/ppermute | solution.py:142
  16.0 12.9 %collective-permute-start.3 = (f32[80,896]{1,0:T(8,128)S(1)}, f32[80,896]{1,0:T(8,128)S(1)}, u32[]{:S(2)}, u32[]{:S(2)}) collective-permute-start(f32[80,896]{1,0:T(8,128)S(1)} %get-tuple-element.20), channel_id=1, source_target_pairs={{0,64},{1,449},{64,0},{65,129},{128,192},{129,65},{192,128},{193,2... | collective-permute-start | bytes 860168 | tf_op jit(solution)/shard_map/ppermute | solution.py:142
  20.7 16.0 %collective-permute-start.5 = (f32[80,896]{1,0:T(8,128)S(1)}, f32[80,896]{1,0:T(8,128)S(1)}, u32[]{:S(2)}, u32[]{:S(2)}) collective-permute-start(f32[80,896]{1,0:T(8,128)S(1)} %add.114), channel_id=1, source_target_pairs={{0,384},{1,129},{64,192},{65,449},{128,0},{129,257},{192,320},{193... | collective-permute-start | bytes 860168 | tf_op jit(solution)/shard_map/ppermute | solution.py:142
  22.6 16.0 %collective-permute-start = (f32[80,896]{1,0:T(8,128)S(1)}, f32[80,896]{1,0:T(8,128)S(1)}, u32[]{:S(2)}, u32[]{:S(2)}) collective-permute-start(f32[80,896]{1,0:T(8,128)S(1)} %get-tuple-element.16), channel_id=1, source_target_pairs={{0,64},{1,449},{64,0},{65,129},{128,192},{129,65},{192,128},{193,2... | collective-permute-start | bytes 860168 | tf_op jit(solution)/shard_map/ppermute | solution.py:142
  24.8 17.6 %collective-permute-start.2 = (f32[80,896]{1,0:T(8,128)S(1)}, f32[80,896]{1,0:T(8,128)S(1)}, u32[]{:S(2)}, u32[]{:S(2)}) collective-permute-start(f32[80,896]{1,0:T(8,128)S(1)} %add.112), channel_id=1, source_target_pairs={{0,384},{1,129},{64,192},{65,449},{128,0},{129,257},{192,320},{193... | collective-permute-start | bytes 860168 | tf_op jit(solution)/shard_map/ppermute | solution.py:142
  36.7 7.7 %collective-permute-start.6 = (f32[80,896]{1,0:T(8,128)S(1)}, f32[80,896]{1,0:T(8,128)S(1)}, u32[]{:S(2)}, u32[]{:S(2)}) collective-permute-start(f32[80,896]{1,0:T(8,128)S(1)} %add_add_fusion), channel_id=1, source_target_pairs={{0,448},{1,65},{64,128},{65,1},{128,64},{129,193},{192,256},{193,1... | collective-permute-start | bytes 860168 | tf_op jit(solution)/shard_map/ppermute | solution.py:142

commit v6 on v5

--- a/solution.py
+++ b/solution.py
@@ -54,6 +54,21 @@
     return lax.dot_general(
         a, b, (contract, ((), ())), precision=highest, preferred_element_type=jnp.float32
     )
+
+
+def thirds(value):
+    high = value.astype(jnp.bfloat16)
+    rest = value - high.astype(jnp.float32)
+    middle = rest.astype(jnp.bfloat16)
+    return high, middle, (rest - middle.astype(jnp.float32)).astype(jnp.bfloat16)
+
+
+def joined_dot(a, b):
+    a0, a1, a2 = a
+    b0, b1, b2 = b
+    left = jnp.concatenate([a0, a1, a0, a2, a1, a0], axis=1)
+    right = jnp.concatenate([b0, b0, b1, b0, b1, b2], axis=0)
+    return lax.dot_general(left, right, (((1,), (0,)), ((), ())), preferred_element_type=jnp.float32)
 
 
 def momentum_and_gram(*refs):
@@ -89,10 +104,12 @@
     eye = jnp.where(i == j, quintic_a, 0.0)
     product = None
     for iteration in range(ITERS):
-        polynomial = eye + quintic_b * square + quintic_c * dot(square, square)
-        product = polynomial if product is None else dot(product, polynomial)
+        terms = thirds(square)
+        polynomial = eye + quintic_b * square + quintic_c * joined_dot(terms, terms)
+        factors = thirds(polynomial)
+        product = polynomial if product is None else joined_dot(thirds(product), factors)
         if iteration < ITERS - 1:
-            square = dot(dot(square, polynomial), polynomial)
+            square = joined_dot(thirds(joined_dot(terms, factors)), factors)
     factor = 0.2 * math.sqrt(max(HEAD_DIM, COLS))
     body, diagonal = pack(product * (factor * scale))
     out_ref[:HALF] = body
@@ -145,8 +162,9 @@
     chunks = dict(zip(offsets, lax.optimization_barrier(tuple(chunk(k) for k in offsets))))
     fourth, third, second = (send(chunks[k], 1) for k in (4, 3, 2))
     relayed = send(chunks[-3] + fourth, -2)
+    to_second, chunks[1] = lax.optimization_barrier((chunks[-2] + third, chunks[1]))
+    from_second = send(to_second, -2)
     partner = send(chunks[1], 1)
-    from_second = send(chunks[-2] + third, -2)
     from_first = send(chunks[-1] + second + relayed, -1)
     return chunks[0], partner, from_second, from_first
 

time: 91.9 us -> 91.4 us (level)
    all_gather x1, blocking collectives: 3.53 us -> 2.47 us  [on_device(): both = lax.all_gather(gram, 'core')]
  transfers between devices with their start and end apart: 7 -> 7, of which waited for: 3 -> 4; matrix products, arithmetic and copies ran while one was open for 0% -> 0% of each run, Pallas kernels for 0% -> 0%
where the time goes in v6:
time: 91.4 us; the launch traced here: 91 us
  blocking collectives  41.4 us (45%)
  starting transfers between devices  28.2 us (31%)
  waiting for transfers between devices  13.4 us (15%)
  Pallas kernels  5.16 us (6%)
  local copies, waits for them, and re-layouts  1.79 us (2%)
    ppermute x7, starting transfers between devices, send(): return lax.ppermute(value, ('replica', 'core'), pairs)  28.2 us
    all_to_all x1, blocking collectives, on_device(): parts = lax.all_to_all(parts, 'y', split_axis=0, concat_axis=0, tiled=True)  16 us
    all_to_all x1, blocking collectives, on_device(): lax.all_to_all(products, OWNERS, split_axis=0, concat_axis=0, tiled=True)  14 us
    ppermute x7, waiting for transfers between devices, send(): return lax.ppermute(value, ('replica', 'core'), pairs)  13.4 us
    all_to_all x1, blocking collectives, on_device(): lax.all_to_all(jnp.sum(mine, axis=0), 'x', split_axis=0, concat_axis=0, t...  8.99 us
    pallas_call x1, Pallas kernels, on_device(): pl.pallas_call(newton_schulz, in_specs=[pl.BlockSpec(memory_space=pltpu.V...  3.1 us
    all_gather x1, blocking collectives, on_device(): both = lax.all_gather(gram, 'core')  2.47 us
  transfers between devices with their start and end apart: 7, of which 4 were waited for; matrix products, arithmetic and copies ran while one was open for 0% of the time, Pallas kernels for 0%

profile of v6, /device:TPU:1, one launch (start us, length us, event | category | flops | bytes accessed | tf_op | source)
XLA Modules:
  0.0 91.0 jit_solution(3983323688724988755)
XLA Ops:
  0.7 1.7 %dynamic-slice_bitcast_fusion = (f32[80,896]{1,0:T(8,128)S(1)}, f32[80,896]{1,0:T(8,128)S(1)}, f32[80,896]{1,0:T(8,128)S(1)}, f32[80,896]{1,0:T(8,128)S(1)}, f32...) fusion(f32[1,80,7168]{2,1,0:T(8,128)} %param.2, s32[]{:T(128)S(6)} %select_n.35, ...), kind=kLoop, calls=%fused_computation.2 | loop fusion | bytes 4587552 | tf_op jit(solution)/shard_map/dynamic_slice | solution.py:149
  2.4 0.0 copy-start
  2.5 11.6 %collective-permute-start.4 = (f32[80,896]{1,0:T(8,128)S(1)}, f32[80,896]{1,0:T(8,128)S(1)}, u32[]{:S(2)}, u32[]{:S(2)}) collective-permute-start(f32[80,896]{1,0:T(8,128)S(1)} %get-tuple-element.26), channel_id=1, source_target_pairs={{0,64},{1,449},{64,0},{65,129},{128,192},{129,65},{192,128},{193,2... | collective-permute-start | bytes 860168 | tf_op jit(solution)/shard_map/ppermute | solution.py:159
  14.1 1.9 %collective-permute-start = (f32[80,896]{1,0:T(8,128)S(1)}, f32[80,896]{1,0:T(8,128)S(1)}, u32[]{:S(2)}, u32[]{:S(2)}) collective-permute-start(f32[80,896]{1,0:T(8,128)S(1)} %get-tuple-element.19), channel_id=1, source_target_pairs={{0,64},{1,449},{64,0},{65,129},{128,192},{129,65},{192,128},{193,2... | collective-permute-start | bytes 860168 | tf_op jit(solution)/shard_map/ppermute | solution.py:159
  16.0 4.6 %collective-permute-start.3 = (f32[80,896]{1,0:T(8,128)S(1)}, f32[80,896]{1,0:T(8,128)S(1)}, u32[]{:S(2)}, u32[]{:S(2)}) collective-permute-start(f32[80,896]{1,0:T(8,128)S(1)} %get-tuple-element.24), channel_id=1, source_target_pairs={{0,64},{1,449},{64,0},{65,129},{128,192},{129,65},{192,128},{193,2... | collective-permute-start | bytes 860168 | tf_op jit(solution)/shard_map/ppermute | solution.py:159
  20.6 0.0 collective-permute-done.4
  20.7 1.9 %collective-permute-start.5 = (f32[80,896]{1,0:T(8,128)S(1)}, f32[80,896]{1,0:T(8,128)S(1)}, u32[]{:S(2)}, u32[]{:S(2)}) collective-permute-start(f32[80,896]{1,0:T(8,128)S(1)} %add.114), channel_id=1, source_target_pairs={{0,384},{1,129},{64,192},{65,449},{128,0},{129,257},{192,320},{193... | collective-permute-start | bytes 860168 | tf_op jit(solution)/shard_map/ppermute | solution.py:159
  22.6 0.1 collective-permute-done
  22.7 3.1 %collective-permute-start.1 = (f32[80,896]{1,0:T(8,128)S(1)}, f32[80,896]{1,0:T(8,128)S(1)}, u32[]{:S(2)}, u32[]{:S(2)}) collective-permute-start(f32[80,896]{1,0:T(8,128)S(1)} %get-tuple-element.21), channel_id=1, source_target_pairs={{0,64},{1,449},{64,0},{65,129},{128,192},{129,65},{192,128},{193,2... | collective-permute-start | bytes 860168 | tf_op jit(solution)/shard_map/ppermute | solution.py:159
  25.8 3.2 %collective-permute-start.2 = (f32[80,896]{1,0:T(8,128)S(1)}, f32[80,896]{1,0:T(8,128)S(1)}, u32[]{:S(2)}, u32[]{:S(2)}) collective-permute-start(f32[80,896]{1,0:T(8,128)S(1)} %add.112), channel_id=1, source_target_pairs={{0,384},{1,129},{64,192},{65,449},{128,0},{129,257},{192,320},{193... | collective-permute-start | bytes 860168 | tf_op jit(solution)/shard_map/ppermute | solution.py:159
  29.0 0.0 collective-permute-done.3
  29.0 7.5 %collective-permute-done.5 = f32[80,896]{1,0:T(8,128)S(1)} collective-permute-done((f32[80,896]{1,0:T(8,128)S(1)}, f32[80,896]{1,0:T(8,128)S(1)}, u32[]{:S(2)}, u32[]{:S(2)}) %collective-permute-start.5) | collective-permute-done | bytes 286752 | tf_op jit(solution)/shard_map/ppermute | solution.py:159
  36.5 0.1 add_add_fusion
  36.6 1.9 %collective-permute-start.6 = (f32[80,896]{1,0:T(8,128)S(1)}, f32[80,896]{1,0:T(8,128)S(1)}, u32[]{:S(2)}, u32[]{:S(2)}) collective-permute-start(f32[80,896]{1,0:T(8,128)S(1)} %add_add_fusion), channel_id=1, source_target_pairs={{0,448},{1,65},{64,128},{65,1},{128,64},{129,193},{192,256},{193,1... | collective-permute-start | bytes 860168 | tf_op jit(solution)/shard_map/ppermute | solution.py:159
  38.5 0.0 collective-permute-done.1.refs_1_
  38.5 3.9 %collective-permute-done.2.refs_2_ = f32[80,896]{1,0:T(8,128)S(1)} collective-permute-done((f32[80,896]{1,0:T(8,128)S(1)}, f32[80,896]{1,0:T(8,128)S(1)}, u32[]{:S(2)}, u32[]{:S(2)}) %collective-permute-start.2) | collective-permute-done | bytes 286752 | tf_op jit(solution)/shard_map/ppermute | solution.py:159
  42.4 1.9 %collective-permute-done.6.refs_3_ = f32[80,896]{1,0:T(8,128)S(1)} collective-permute-done((f32[80,896]{1,0:T(8,128)S(1)}, f32[80,896]{1,0:T(8,128)S(1)}, u32[]{:S(2)}, u32[]{:S(2)}) %collective-permute-start.6) | collective-permute-done | bytes 286752 | tf_op jit(solution)/shard_map/ppermute | solution.py:159
  44.3 0.7 shard_map.41
  45.0 2.5 %all-gather = f32[4,4,72,128]{3,2,1,0:T(8,128)S(1)} all-gather(f32[2,4,72,128]{3,2,1,0:T(8,128)S(1)} %get-tuple-element.28), channel_id=2, replica_groups=mesh['replica'=8,'y'=8,'x'=4,'core'=2] {'core'}, dimensions={0}, use_global_device_ids=true | all-gather | bytes 884736 | tf_op jit(solution)/shard_map/all_gather | solution.py:184
  47.5 9.0 %all_to_all.15 = f32[4,72,128]{2,1,0:T(8,128)S(1)} all-to-all(f32[4,72,128]{2,1,0:T(8,128)S(1)} %dynamic-slice_reduce_fusion), channel_id=1, replica_groups=mesh['replica'=8,'y'=8,'x'=4,'core'=2] {'x'}, dimensions={0} | all-to-all | bytes 294912 | tf_op jit(solution)/shard_map/all_to_all | solution.py:186
  56.5 16.0 %all_to_all.16.parts_ref = f32[8,72,128]{2,1,0:T(8,128)S(1)} all-to-all(f32[8,72,128]{2,1,0:T(8,128)S(1)} %broadcast_in_dim.4), channel_id=1, replica_groups=mesh['replica'=8,'y'=8,'x'=4,'core'=2] {'y'}, dimensions={0} | all-to-all | bytes 589824 | tf_op jit(solution)/shard_map/all_to_all | solution.py:189
  72.4 3.1 %shard_map.42 = (f32[72,128]{1,0:T(8,128)S(1)}, f32[80,896]{1,0:T(8,128)}) custom-call(f32[8,72,128]{2,1,0:T(8,128)S(1)} %all_to_all.16.parts_ref, f32[80,896]{1,0:T(8,128)S(1)} %get-tuple-element.29.next_ref), custom_call_target="tpu_custom_call" | custom-call | tf_op jit(solution)/shard_map/pallas_call | solution.py:190
  75.6 14.0 %all_to_all.17.product_ref = f32[8,72,128]{2,1,0:T(8,128)S(1)} all-to-all(f32[8,72,128]{2,1,0:T(8,128)S(1)} %broadcast_in_dim.5), channel_id=1, replica_groups=mesh['replica'=8,'y'=8,'x'=4,'core'=2] {'x','core'}, dimensions={0} | all-to-all | bytes 589824 | tf_op jit(solution)/shard_map/all_to_all | solution.py:199
  89.6 1.4 %shard_map.43 = f32[80,896]{1,0:T(8,128)} custom-call(f32[80,896]{1,0:T(8,128)S(1)} %get-tuple-element.27.blended_ref, f32[8,72,128]{2,1,0:T(8,128)S(1)} %all_to_all.17.product_ref), custom_call_target="tpu_custom_call" | custom-call | tf_op jit(solution)/shard_map/pallas_call | solution.py:200
  (7 shorter events, 0.1 us)
Async XLA Ops:
  2.4 41.8 %copy-start = (f32[80,896]{1,0:T(8,128)S(1)}, f32[80,896]{1,0:T(8,128)}, u32[]{:S(2)}) copy-start(f32[80,896]{1,0:T(8,128)} %refs_4_.1) | copy-start | bytes 860164
  2.5 18.1 %collective-permute-start.4 = (f32[80,896]{1,0:T(8,128)S(1)}, f32[80,896]{1,0:T(8,128)S(1)}, u32[]{:S(2)}, u32[]{:S(2)}) collective-permute-start(f32[80,896]{1,0:T(8,128)S(1)} %get-tuple-element.26), channel_id=1, source_target_pairs={{0,64},{1,449},{64,0},{65,129},{128,192},{129,65},{192,128},{193,2... | collective-permute-start | bytes 860168 | tf_op jit(solution)/shard_map/ppermute | solution.py:159
  14.1 8.6 %collective-permute-start = (f32[80,896]{1,0:T(8,128)S(1)}, f32[80,896]{1,0:T(8,128)S(1)}, u32[]{:S(2)}, u32[]{:S(2)}) collective-permute-start(f32[80,896]{1,0:T(8,128)S(1)} %get-tuple-element.19), channel_id=1, source_target_pairs={{0,64},{1,449},{64,0},{65,129},{128,192},{129,65},{192,128},{193,2... | collective-permute-start | bytes 860168 | tf_op jit(solution)/shard_map/ppermute | solution.py:159
  16.0 13.0 %collective-permute-start.3 = (f32[80,896]{1,0:T(8,128)S(1)}, f32[80,896]{1,0:T(8,128)S(1)}, u32[]{:S(2)}, u32[]{:S(2)}) collective-permute-start(f32[80,896]{1,0:T(8,128)S(1)} %get-tuple-element.24), channel_id=1, source_target_pairs={{0,64},{1,449},{64,0},{65,129},{128,192},{129,65},{192,128},{193,2... | collective-permute-start | bytes 860168 | tf_op jit(solution)/shard_map/ppermute | solution.py:159
  20.7 15.9 %collective-permute-start.5 = (f32[80,896]{1,0:T(8,128)S(1)}, f32[80,896]{1,0:T(8,128)S(1)}, u32[]{:S(2)}, u32[]{:S(2)}) collective-permute-start(f32[80,896]{1,0:T(8,128)S(1)} %add.114), channel_id=1, source_target_pairs={{0,384},{1,129},{64,192},{65,449},{128,0},{129,257},{192,320},{193... | collective-permute-start | bytes 860168 | tf_op jit(solution)/shard_map/ppermute | solution.py:159
  22.7 15.8 %collective-permute-start.1 = (f32[80,896]{1,0:T(8,128)S(1)}, f32[80,896]{1,0:T(8,128)S(1)}, u32[]{:S(2)}, u32[]{:S(2)}) collective-permute-start(f32[80,896]{1,0:T(8,128)S(1)} %get-tuple-element.21), channel_id=1, source_target_pairs={{0,64},{1,449},{64,0},{65,129},{128,192},{129,65},{192,128},{193,2... | collective-permute-start | bytes 860168 | tf_op jit(solution)/shard_map/ppermute | solution.py:159
  25.8 16.6 %collective-permute-start.2 = (f32[80,896]{1,0:T(8,128)S(1)}, f32[80,896]{1,0:T(8,128)S(1)}, u32[]{:S(2)}, u32[]{:S(2)}) collective-permute-start(f32[80,896]{1,0:T(8,128)S(1)} %add.112), channel_id=1, source_target_pairs={{0,384},{1,129},{64,192},{65,449},{128,0},{129,257},{192,320},{193... | collective-permute-start | bytes 860168 | tf_op jit(solution)/shard_map/ppermute | solution.py:159
  36.6 7.7 %collective-permute-start.6 = (f32[80,896]{1,0:T(8,128)S(1)}, f32[80,896]{1,0:T(8,128)S(1)}, u32[]{:S(2)}, u32[]{:S(2)}) collective-permute-start(f32[80,896]{1,0:T(8,128)S(1)} %add_add_fusion), channel_id=1, source_target_pairs={{0,448},{1,65},{64,128},{65,1},{128,64},{129,193},{192,256},{193,1... | collective-permute-start | bytes 860168 | tf_op jit(solution)/shard_map/ppermute | solution.py:159

commit v7 on v6

--- a/solution.py
+++ b/solution.py
@@ -110,6 +110,7 @@
         product = polynomial if product is None else joined_dot(thirds(product), factors)
         if iteration < ITERS - 1:
             square = joined_dot(thirds(joined_dot(terms, factors)), factors)
+            square = 0.5 * (square + square.T)
     factor = 0.2 * math.sqrt(max(HEAD_DIM, COLS))
     body, diagonal = pack(product * (factor * scale))
     out_ref[:HALF] = body

time: 91.4 us -> 91.7 us (level)
  no operation moved by 1% of the time
where the time goes in v7:
time: 91.7 us; the launch traced here: 91.2 us
  blocking collectives  41.4 us (45%)
  starting transfers between devices  28.2 us (31%)
  waiting for transfers between devices  13.4 us (15%)
  Pallas kernels  5.43 us (6%)
  local copies, waits for them, and re-layouts  1.79 us (2%)
    ppermute x7, starting transfers between devices, send(): return lax.ppermute(value, ('replica', 'core'), pairs)  28.2 us
    all_to_all x1, blocking collectives, on_device(): parts = lax.all_to_all(parts, 'y', split_axis=0, concat_axis=0, tiled=True)  16 us
    all_to_all x1, blocking collectives, on_device(): lax.all_to_all(products, OWNERS, split_axis=0, concat_axis=0, tiled=True)  14 us
    ppermute x7, waiting for transfers between devices, send(): return lax.ppermute(value, ('replica', 'core'), pairs)  13.4 us
    all_to_all x1, blocking collectives, on_device(): lax.all_to_all(jnp.sum(mine, axis=0), 'x', split_axis=0, concat_axis=0, t...  8.99 us
    pallas_call x1, Pallas kernels, on_device(): pl.pallas_call(newton_schulz, in_specs=[pl.BlockSpec(memory_space=pltpu.V...  3.38 us
    all_gather x1, blocking collectives, on_device(): both = lax.all_gather(gram, 'core')  2.47 us
  transfers between devices with their start and end apart: 7, of which 4 were waited for; matrix products, arithmetic and copies ran while one was open for 0% of the time, Pallas kernels for 0%

profile of v7, /device:TPU:1, one launch (start us, length us, event | category | flops | bytes accessed | tf_op | source)
XLA Modules:
  0.0 91.2 jit_solution(9638925426566059921)
XLA Ops:
  0.7 1.7 %dynamic-slice_bitcast_fusion = (f32[80,896]{1,0:T(8,128)S(1)}, f32[80,896]{1,0:T(8,128)S(1)}, f32[80,896]{1,0:T(8,128)S(1)}, f32[80,896]{1,0:T(8,128)S(1)}, f32...) fusion(f32[1,80,7168]{2,1,0:T(8,128)} %param.2, s32[]{:T(128)S(6)} %select_n.35, ...), kind=kLoop, calls=%fused_computation.2 | loop fusion | bytes 4587552 | tf_op jit(solution)/shard_map/dynamic_slice | solution.py:150
  2.4 0.0 copy-start
  2.5 11.6 %collective-permute-start.4 = (f32[80,896]{1,0:T(8,128)S(1)}, f32[80,896]{1,0:T(8,128)S(1)}, u32[]{:S(2)}, u32[]{:S(2)}) collective-permute-start(f32[80,896]{1,0:T(8,128)S(1)} %get-tuple-element.26), channel_id=1, source_target_pairs={{0,64},{1,449},{64,0},{65,129},{128,192},{129,65},{192,128},{193,2... | collective-permute-start | bytes 860168 | tf_op jit(solution)/shard_map/ppermute | solution.py:160
  14.1 1.9 %collective-permute-start = (f32[80,896]{1,0:T(8,128)S(1)}, f32[80,896]{1,0:T(8,128)S(1)}, u32[]{:S(2)}, u32[]{:S(2)}) collective-permute-start(f32[80,896]{1,0:T(8,128)S(1)} %get-tuple-element.19), channel_id=1, source_target_pairs={{0,64},{1,449},{64,0},{65,129},{128,192},{129,65},{192,128},{193,2... | collective-permute-start | bytes 860168 | tf_op jit(solution)/shard_map/ppermute | solution.py:160
  16.0 4.6 %collective-permute-start.3 = (f32[80,896]{1,0:T(8,128)S(1)}, f32[80,896]{1,0:T(8,128)S(1)}, u32[]{:S(2)}, u32[]{:S(2)}) collective-permute-start(f32[80,896]{1,0:T(8,128)S(1)} %get-tuple-element.24), channel_id=1, source_target_pairs={{0,64},{1,449},{64,0},{65,129},{128,192},{129,65},{192,128},{193,2... | collective-permute-start | bytes 860168 | tf_op jit(solution)/shard_map/ppermute | solution.py:160
  20.6 0.0 collective-permute-done.4
  20.7 1.9 %collective-permute-start.5 = (f32[80,896]{1,0:T(8,128)S(1)}, f32[80,896]{1,0:T(8,128)S(1)}, u32[]{:S(2)}, u32[]{:S(2)}) collective-permute-start(f32[80,896]{1,0:T(8,128)S(1)} %add.114), channel_id=1, source_target_pairs={{0,384},{1,129},{64,192},{65,449},{128,0},{129,257},{192,320},{193... | collective-permute-start | bytes 860168 | tf_op jit(solution)/shard_map/ppermute | solution.py:160
  22.6 0.1 collective-permute-done
  22.7 3.1 %collective-permute-start.1 = (f32[80,896]{1,0:T(8,128)S(1)}, f32[80,896]{1,0:T(8,128)S(1)}, u32[]{:S(2)}, u32[]{:S(2)}) collective-permute-start(f32[80,896]{1,0:T(8,128)S(1)} %get-tuple-element.21), channel_id=1, source_target_pairs={{0,64},{1,449},{64,0},{65,129},{128,192},{129,65},{192,128},{193,2... | collective-permute-start | bytes 860168 | tf_op jit(solution)/shard_map/ppermute | solution.py:160
  25.8 3.2 %collective-permute-start.2 = (f32[80,896]{1,0:T(8,128)S(1)}, f32[80,896]{1,0:T(8,128)S(1)}, u32[]{:S(2)}, u32[]{:S(2)}) collective-permute-start(f32[80,896]{1,0:T(8,128)S(1)} %add.112), channel_id=1, source_target_pairs={{0,384},{1,129},{64,192},{65,449},{128,0},{129,257},{192,320},{193... | collective-permute-start | bytes 860168 | tf_op jit(solution)/shard_map/ppermute | solution.py:160
  29.0 0.0 collective-permute-done.3
  29.0 7.5 %collective-permute-done.5 = f32[80,896]{1,0:T(8,128)S(1)} collective-permute-done((f32[80,896]{1,0:T(8,128)S(1)}, f32[80,896]{1,0:T(8,128)S(1)}, u32[]{:S(2)}, u32[]{:S(2)}) %collective-permute-start.5) | collective-permute-done | bytes 286752 | tf_op jit(solution)/shard_map/ppermute | solution.py:160
  36.5 0.1 add_add_fusion
  36.6 1.9 %collective-permute-start.6 = (f32[80,896]{1,0:T(8,128)S(1)}, f32[80,896]{1,0:T(8,128)S(1)}, u32[]{:S(2)}, u32[]{:S(2)}) collective-permute-start(f32[80,896]{1,0:T(8,128)S(1)} %add_add_fusion), channel_id=1, source_target_pairs={{0,448},{1,65},{64,128},{65,1},{128,64},{129,193},{192,256},{193,1... | collective-permute-start | bytes 860168 | tf_op jit(solution)/shard_map/ppermute | solution.py:160
  38.5 0.0 collective-permute-done.1.refs_1_
  38.5 3.9 %collective-permute-done.2.refs_2_ = f32[80,896]{1,0:T(8,128)S(1)} collective-permute-done((f32[80,896]{1,0:T(8,128)S(1)}, f32[80,896]{1,0:T(8,128)S(1)}, u32[]{:S(2)}, u32[]{:S(2)}) %collective-permute-start.2) | collective-permute-done | bytes 286752 | tf_op jit(solution)/shard_map/ppermute | solution.py:160
  42.4 1.9 %collective-permute-done.6.refs_3_ = f32[80,896]{1,0:T(8,128)S(1)} collective-permute-done((f32[80,896]{1,0:T(8,128)S(1)}, f32[80,896]{1,0:T(8,128)S(1)}, u32[]{:S(2)}, u32[]{:S(2)}) %collective-permute-start.6) | collective-permute-done | bytes 286752 | tf_op jit(solution)/shard_map/ppermute | solution.py:160
  44.3 0.7 shard_map.41
  45.0 2.5 %all-gather = f32[4,4,72,128]{3,2,1,0:T(8,128)S(1)} all-gather(f32[2,4,72,128]{3,2,1,0:T(8,128)S(1)} %get-tuple-element.28), channel_id=2, replica_groups=mesh['replica'=8,'y'=8,'x'=4,'core'=2] {'core'}, dimensions={0}, use_global_device_ids=true | all-gather | bytes 884736 | tf_op jit(solution)/shard_map/all_gather | solution.py:185
  47.5 9.0 %all_to_all.15 = f32[4,72,128]{2,1,0:T(8,128)S(1)} all-to-all(f32[4,72,128]{2,1,0:T(8,128)S(1)} %dynamic-slice_reduce_fusion), channel_id=1, replica_groups=mesh['replica'=8,'y'=8,'x'=4,'core'=2] {'x'}, dimensions={0} | all-to-all | bytes 294912 | tf_op jit(solution)/shard_map/all_to_all | solution.py:187
  56.5 16.0 %all_to_all.16.parts_ref = f32[8,72,128]{2,1,0:T(8,128)S(1)} all-to-all(f32[8,72,128]{2,1,0:T(8,128)S(1)} %broadcast_in_dim.4), channel_id=1, replica_groups=mesh['replica'=8,'y'=8,'x'=4,'core'=2] {'y'}, dimensions={0} | all-to-all | bytes 589824 | tf_op jit(solution)/shard_map/all_to_all | solution.py:190
  72.4 3.4 %shard_map.42 = (f32[72,128]{1,0:T(8,128)S(1)}, f32[80,896]{1,0:T(8,128)}) custom-call(f32[8,72,128]{2,1,0:T(8,128)S(1)} %all_to_all.16.parts_ref, f32[80,896]{1,0:T(8,128)S(1)} %get-tuple-element.29.next_ref), custom_call_target="tpu_custom_call" | custom-call | tf_op jit(solution)/shard_map/pallas_call | solution.py:191
  75.9 14.0 %all_to_all.17.product_ref = f32[8,72,128]{2,1,0:T(8,128)S(1)} all-to-all(f32[8,72,128]{2,1,0:T(8,128)S(1)} %broadcast_in_dim.5), channel_id=1, replica_groups=mesh['replica'=8,'y'=8,'x'=4,'core'=2] {'x','core'}, dimensions={0} | all-to-all | bytes 589824 | tf_op jit(solution)/shard_map/all_to_all | solution.py:200
  89.9 1.4 %shard_map.43 = f32[80,896]{1,0:T(8,128)} custom-call(f32[80,896]{1,0:T(8,128)S(1)} %get-tuple-element.27.blended_ref, f32[8,72,128]{2,1,0:T(8,128)S(1)} %all_to_all.17.product_ref), custom_call_target="tpu_custom_call" | custom-call | tf_op jit(solution)/shard_map/pallas_call | solution.py:201
  (7 shorter events, 0.1 us)
Async XLA Ops:
  2.4 41.8 %copy-start = (f32[80,896]{1,0:T(8,128)S(1)}, f32[80,896]{1,0:T(8,128)}, u32[]{:S(2)}) copy-start(f32[80,896]{1,0:T(8,128)} %refs_4_.1) | copy-start | bytes 860164
  2.5 18.1 %collective-permute-start.4 = (f32[80,896]{1,0:T(8,128)S(1)}, f32[80,896]{1,0:T(8,128)S(1)}, u32[]{:S(2)}, u32[]{:S(2)}) collective-permute-start(f32[80,896]{1,0:T(8,128)S(1)} %get-tuple-element.26), channel_id=1, source_target_pairs={{0,64},{1,449},{64,0},{65,129},{128,192},{129,65},{192,128},{193,2... | collective-permute-start | bytes 860168 | tf_op jit(solution)/shard_map/ppermute | solution.py:160
  14.1 8.6 %collective-permute-start = (f32[80,896]{1,0:T(8,128)S(1)}, f32[80,896]{1,0:T(8,128)S(1)}, u32[]{:S(2)}, u32[]{:S(2)}) collective-permute-start(f32[80,896]{1,0:T(8,128)S(1)} %get-tuple-element.19), channel_id=1, source_target_pairs={{0,64},{1,449},{64,0},{65,129},{128,192},{129,65},{192,128},{193,2... | collective-permute-start | bytes 860168 | tf_op jit(solution)/shard_map/ppermute | solution.py:160
  16.0 13.0 %collective-permute-start.3 = (f32[80,896]{1,0:T(8,128)S(1)}, f32[80,896]{1,0:T(8,128)S(1)}, u32[]{:S(2)}, u32[]{:S(2)}) collective-permute-start(f32[80,896]{1,0:T(8,128)S(1)} %get-tuple-element.24), channel_id=1, source_target_pairs={{0,64},{1,449},{64,0},{65,129},{128,192},{129,65},{192,128},{193,2... | collective-permute-start | bytes 860168 | tf_op jit(solution)/shard_map/ppermute | solution.py:160
  20.7 15.9 %collective-permute-start.5 = (f32[80,896]{1,0:T(8,128)S(1)}, f32[80,896]{1,0:T(8,128)S(1)}, u32[]{:S(2)}, u32[]{:S(2)}) collective-permute-start(f32[80,896]{1,0:T(8,128)S(1)} %add.114), channel_id=1, source_target_pairs={{0,384},{1,129},{64,192},{65,449},{128,0},{129,257},{192,320},{193... | collective-permute-start | bytes 860168 | tf_op jit(solution)/shard_map/ppermute | solution.py:160
  22.7 15.8 %collective-permute-start.1 = (f32[80,896]{1,0:T(8,128)S(1)}, f32[80,896]{1,0:T(8,128)S(1)}, u32[]{:S(2)}, u32[]{:S(2)}) collective-permute-start(f32[80,896]{1,0:T(8,128)S(1)} %get-tuple-element.21), channel_id=1, source_target_pairs={{0,64},{1,449},{64,0},{65,129},{128,192},{129,65},{192,128},{193,2... | collective-permute-start | bytes 860168 | tf_op jit(solution)/shard_map/ppermute | solution.py:160
  25.8 16.6 %collective-permute-start.2 = (f32[80,896]{1,0:T(8,128)S(1)}, f32[80,896]{1,0:T(8,128)S(1)}, u32[]{:S(2)}, u32[]{:S(2)}) collective-permute-start(f32[80,896]{1,0:T(8,128)S(1)} %add.112), channel_id=1, source_target_pairs={{0,384},{1,129},{64,192},{65,449},{128,0},{129,257},{192,320},{193... | collective-permute-start | bytes 860168 | tf_op jit(solution)/shard_map/ppermute | solution.py:160
  36.6 7.7 %collective-permute-start.6 = (f32[80,896]{1,0:T(8,128)S(1)}, f32[80,896]{1,0:T(8,128)S(1)}, u32[]{:S(2)}, u32[]{:S(2)}) collective-permute-start(f32[80,896]{1,0:T(8,128)S(1)} %add_add_fusion), channel_id=1, source_target_pairs={{0,448},{1,65},{64,128},{65,1},{128,64},{129,193},{192,256},{193,1... | collective-permute-start | bytes 860168 | tf_op jit(solution)/shard_map/ppermute | solution.py:160

commit v8 on v6

--- a/solution.py
+++ b/solution.py
@@ -110,6 +110,8 @@
         product = polynomial if product is None else joined_dot(thirds(product), factors)
         if iteration < ITERS - 1:
             square = joined_dot(thirds(joined_dot(terms, factors)), factors)
+            if iteration < 2:
+                square = 0.5 * (square + square.T)
     factor = 0.2 * math.sqrt(max(HEAD_DIM, COLS))
     body, diagonal = pack(product * (factor * scale))
     out_ref[:HALF] = body

time: 91.4 us -> 91.5 us (level)
  no operation moved by 1% of the time
where the time goes in v8:
time: 91.5 us; the launch traced here: 91.1 us
  blocking collectives  41.4 us (45%)
  starting transfers between devices  28.2 us (31%)
  waiting for transfers between devices  13.4 us (15%)
  Pallas kernels  5.3 us (6%)
  local copies, waits for them, and re-layouts  1.79 us (2%)
    ppermute x7, starting transfers between devices, send(): return lax.ppermute(value, ('replica', 'core'), pairs)  28.2 us
    all_to_all x1, blocking collectives, on_device(): parts = lax.all_to_all(parts, 'y', split_axis=0, concat_axis=0, tiled=True)  16 us
    all_to_all x1, blocking collectives, on_device(): lax.all_to_all(products, OWNERS, split_axis=0, concat_axis=0, tiled=True)  14 us
    ppermute x7, waiting for transfers between devices, send(): return lax.ppermute(value, ('replica', 'core'), pairs)  13.4 us
    all_to_all x1, blocking collectives, on_device(): lax.all_to_all(jnp.sum(mine, axis=0), 'x', split_axis=0, concat_axis=0, t...  8.99 us
    pallas_call x1, Pallas kernels, on_device(): pl.pallas_call(newton_schulz, in_specs=[pl.BlockSpec(memory_space=pltpu.V...  3.25 us
    all_gather x1, blocking collectives, on_device(): both = lax.all_gather(gram, 'core')  2.47 us
  transfers between devices with their start and end apart: 7, of which 4 were waited for; matrix products, arithmetic and copies ran while one was open for 0% of the time, Pallas kernels for 0%

profile of v8, /device:TPU:1, one launch (start us, length us, event | category | flops | bytes accessed | tf_op | source)
XLA Modules:
  0.0 91.1 jit_solution(11928956856242893849)
XLA Ops:
  0.7 1.7 %dynamic-slice_bitcast_fusion = (f32[80,896]{1,0:T(8,128)S(1)}, f32[80,896]{1,0:T(8,128)S(1)}, f32[80,896]{1,0:T(8,128)S(1)}, f32[80,896]{1,0:T(8,128)S(1)}, f32...) fusion(f32[1,80,7168]{2,1,0:T(8,128)} %param.2, s32[]{:T(128)S(6)} %select_n.35, ...), kind=kLoop, calls=%fused_computation.2 | loop fusion | bytes 4587552 | tf_op jit(solution)/shard_map/dynamic_slice | solution.py:151
  2.4 0.0 copy-start
  2.5 11.6 %collective-permute-start.4 = (f32[80,896]{1,0:T(8,128)S(1)}, f32[80,896]{1,0:T(8,128)S(1)}, u32[]{:S(2)}, u32[]{:S(2)}) collective-permute-start(f32[80,896]{1,0:T(8,128)S(1)} %get-tuple-element.26), channel_id=1, source_target_pairs={{0,64},{1,449},{64,0},{65,129},{128,192},{129,65},{192,128},{193,2... | collective-permute-start | bytes 860168 | tf_op jit(solution)/shard_map/ppermute | solution.py:161
  14.1 1.9 %collective-permute-start = (f32[80,896]{1,0:T(8,128)S(1)}, f32[80,896]{1,0:T(8,128)S(1)}, u32[]{:S(2)}, u32[]{:S(2)}) collective-permute-start(f32[80,896]{1,0:T(8,128)S(1)} %get-tuple-element.19), channel_id=1, source_target_pairs={{0,64},{1,449},{64,0},{65,129},{128,192},{129,65},{192,128},{193,2... | collective-permute-start | bytes 860168 | tf_op jit(solution)/shard_map/ppermute | solution.py:161
  16.0 4.6 %collective-permute-start.3 = (f32[80,896]{1,0:T(8,128)S(1)}, f32[80,896]{1,0:T(8,128)S(1)}, u32[]{:S(2)}, u32[]{:S(2)}) collective-permute-start(f32[80,896]{1,0:T(8,128)S(1)} %get-tuple-element.24), channel_id=1, source_target_pairs={{0,64},{1,449},{64,0},{65,129},{128,192},{129,65},{192,128},{193,2... | collective-permute-start | bytes 860168 | tf_op jit(solution)/shard_map/ppermute | solution.py:161
  20.6 0.0 collective-permute-done.4
  20.7 1.9 %collective-permute-start.5 = (f32[80,896]{1,0:T(8,128)S(1)}, f32[80,896]{1,0:T(8,128)S(1)}, u32[]{:S(2)}, u32[]{:S(2)}) collective-permute-start(f32[80,896]{1,0:T(8,128)S(1)} %add.114), channel_id=1, source_target_pairs={{0,384},{1,129},{64,192},{65,449},{128,0},{129,257},{192,320},{193... | collective-permute-start | bytes 860168 | tf_op jit(solution)/shard_map/ppermute | solution.py:161
  22.6 0.1 collective-permute-done
  22.7 3.1 %collective-permute-start.1 = (f32[80,896]{1,0:T(8,128)S(1)}, f32[80,896]{1,0:T(8,128)S(1)}, u32[]{:S(2)}, u32[]{:S(2)}) collective-permute-start(f32[80,896]{1,0:T(8,128)S(1)} %get-tuple-element.21), channel_id=1, source_target_pairs={{0,64},{1,449},{64,0},{65,129},{128,192},{129,65},{192,128},{193,2... | collective-permute-start | bytes 860168 | tf_op jit(solution)/shard_map/ppermute | solution.py:161
  25.8 3.2 %collective-permute-start.2 = (f32[80,896]{1,0:T(8,128)S(1)}, f32[80,896]{1,0:T(8,128)S(1)}, u32[]{:S(2)}, u32[]{:S(2)}) collective-permute-start(f32[80,896]{1,0:T(8,128)S(1)} %add.112), channel_id=1, source_target_pairs={{0,384},{1,129},{64,192},{65,449},{128,0},{129,257},{192,320},{193... | collective-permute-start | bytes 860168 | tf_op jit(solution)/shard_map/ppermute | solution.py:161
  29.0 0.0 collective-permute-done.3
  29.0 7.5 %collective-permute-done.5 = f32[80,896]{1,0:T(8,128)S(1)} collective-permute-done((f32[80,896]{1,0:T(8,128)S(1)}, f32[80,896]{1,0:T(8,128)S(1)}, u32[]{:S(2)}, u32[]{:S(2)}) %collective-permute-start.5) | collective-permute-done | bytes 286752 | tf_op jit(solution)/shard_map/ppermute | solution.py:161
  36.5 0.1 add_add_fusion
  36.6 1.9 %collective-permute-start.6 = (f32[80,896]{1,0:T(8,128)S(1)}, f32[80,896]{1,0:T(8,128)S(1)}, u32[]{:S(2)}, u32[]{:S(2)}) collective-permute-start(f32[80,896]{1,0:T(8,128)S(1)} %add_add_fusion), channel_id=1, source_target_pairs={{0,448},{1,65},{64,128},{65,1},{128,64},{129,193},{192,256},{193,1... | collective-permute-start | bytes 860168 | tf_op jit(solution)/shard_map/ppermute | solution.py:161
  38.5 0.0 collective-permute-done.1.refs_1_
  38.5 3.9 %collective-permute-done.2.refs_2_ = f32[80,896]{1,0:T(8,128)S(1)} collective-permute-done((f32[80,896]{1,0:T(8,128)S(1)}, f32[80,896]{1,0:T(8,128)S(1)}, u32[]{:S(2)}, u32[]{:S(2)}) %collective-permute-start.2) | collective-permute-done | bytes 286752 | tf_op jit(solution)/shard_map/ppermute | solution.py:161
  42.4 1.9 %collective-permute-done.6.refs_3_ = f32[80,896]{1,0:T(8,128)S(1)} collective-permute-done((f32[80,896]{1,0:T(8,128)S(1)}, f32[80,896]{1,0:T(8,128)S(1)}, u32[]{:S(2)}, u32[]{:S(2)}) %collective-permute-start.6) | collective-permute-done | bytes 286752 | tf_op jit(solution)/shard_map/ppermute | solution.py:161
  44.3 0.7 shard_map.41
  45.0 2.5 %all-gather = f32[4,4,72,128]{3,2,1,0:T(8,128)S(1)} all-gather(f32[2,4,72,128]{3,2,1,0:T(8,128)S(1)} %get-tuple-element.28), channel_id=2, replica_groups=mesh['replica'=8,'y'=8,'x'=4,'core'=2] {'core'}, dimensions={0}, use_global_device_ids=true | all-gather | bytes 884736 | tf_op jit(solution)/shard_map/all_gather | solution.py:186
  47.5 9.0 %all_to_all.15 = f32[4,72,128]{2,1,0:T(8,128)S(1)} all-to-all(f32[4,72,128]{2,1,0:T(8,128)S(1)} %dynamic-slice_reduce_fusion), channel_id=1, replica_groups=mesh['replica'=8,'y'=8,'x'=4,'core'=2] {'x'}, dimensions={0} | all-to-all | bytes 294912 | tf_op jit(solution)/shard_map/all_to_all | solution.py:188
  56.5 16.0 %all_to_all.16.parts_ref = f32[8,72,128]{2,1,0:T(8,128)S(1)} all-to-all(f32[8,72,128]{2,1,0:T(8,128)S(1)} %broadcast_in_dim.4), channel_id=1, replica_groups=mesh['replica'=8,'y'=8,'x'=4,'core'=2] {'y'}, dimensions={0} | all-to-all | bytes 589824 | tf_op jit(solution)/shard_map/all_to_all | solution.py:191
  72.4 3.2 %shard_map.42 = (f32[72,128]{1,0:T(8,128)S(1)}, f32[80,896]{1,0:T(8,128)}) custom-call(f32[8,72,128]{2,1,0:T(8,128)S(1)} %all_to_all.16.parts_ref, f32[80,896]{1,0:T(8,128)S(1)} %get-tuple-element.29.next_ref), custom_call_target="tpu_custom_call" | custom-call | tf_op jit(solution)/shard_map/pallas_call | solution.py:192
  75.7 14.0 %all_to_all.17.product_ref = f32[8,72,128]{2,1,0:T(8,128)S(1)} all-to-all(f32[8,72,128]{2,1,0:T(8,128)S(1)} %broadcast_in_dim.5), channel_id=1, replica_groups=mesh['replica'=8,'y'=8,'x'=4,'core'=2] {'x','core'}, dimensions={0} | all-to-all | bytes 589824 | tf_op jit(solution)/shard_map/all_to_all | solution.py:201
  89.7 1.4 %shard_map.43 = f32[80,896]{1,0:T(8,128)} custom-call(f32[80,896]{1,0:T(8,128)S(1)} %get-tuple-element.27.blended_ref, f32[8,72,128]{2,1,0:T(8,128)S(1)} %all_to_all.17.product_ref), custom_call_target="tpu_custom_call" | custom-call | tf_op jit(solution)/shard_map/pallas_call | solution.py:202
  (7 shorter events, 0.1 us)
Async XLA Ops:
  2.4 41.8 %copy-start = (f32[80,896]{1,0:T(8,128)S(1)}, f32[80,896]{1,0:T(8,128)}, u32[]{:S(2)}) copy-start(f32[80,896]{1,0:T(8,128)} %refs_4_.1) | copy-start | bytes 860164
  2.5 18.1 %collective-permute-start.4 = (f32[80,896]{1,0:T(8,128)S(1)}, f32[80,896]{1,0:T(8,128)S(1)}, u32[]{:S(2)}, u32[]{:S(2)}) collective-permute-start(f32[80,896]{1,0:T(8,128)S(1)} %get-tuple-element.26), channel_id=1, source_target_pairs={{0,64},{1,449},{64,0},{65,129},{128,192},{129,65},{192,128},{193,2... | collective-permute-start | bytes 860168 | tf_op jit(solution)/shard_map/ppermute | solution.py:161
  14.1 8.6 %collective-permute-start = (f32[80,896]{1,0:T(8,128)S(1)}, f32[80,896]{1,0:T(8,128)S(1)}, u32[]{:S(2)}, u32[]{:S(2)}) collective-permute-start(f32[80,896]{1,0:T(8,128)S(1)} %get-tuple-element.19), channel_id=1, source_target_pairs={{0,64},{1,449},{64,0},{65,129},{128,192},{129,65},{192,128},{193,2... | collective-permute-start | bytes 860168 | tf_op jit(solution)/shard_map/ppermute | solution.py:161
  16.0 13.0 %collective-permute-start.3 = (f32[80,896]{1,0:T(8,128)S(1)}, f32[80,896]{1,0:T(8,128)S(1)}, u32[]{:S(2)}, u32[]{:S(2)}) collective-permute-start(f32[80,896]{1,0:T(8,128)S(1)} %get-tuple-element.24), channel_id=1, source_target_pairs={{0,64},{1,449},{64,0},{65,129},{128,192},{129,65},{192,128},{193,2... | collective-permute-start | bytes 860168 | tf_op jit(solution)/shard_map/ppermute | solution.py:161
  20.7 15.9 %collective-permute-start.5 = (f32[80,896]{1,0:T(8,128)S(1)}, f32[80,896]{1,0:T(8,128)S(1)}, u32[]{:S(2)}, u32[]{:S(2)}) collective-permute-start(f32[80,896]{1,0:T(8,128)S(1)} %add.114), channel_id=1, source_target_pairs={{0,384},{1,129},{64,192},{65,449},{128,0},{129,257},{192,320},{193... | collective-permute-start | bytes 860168 | tf_op jit(solution)/shard_map/ppermute | solution.py:161
  22.7 15.8 %collective-permute-start.1 = (f32[80,896]{1,0:T(8,128)S(1)}, f32[80,896]{1,0:T(8,128)S(1)}, u32[]{:S(2)}, u32[]{:S(2)}) collective-permute-start(f32[80,896]{1,0:T(8,128)S(1)} %get-tuple-element.21), channel_id=1, source_target_pairs={{0,64},{1,449},{64,0},{65,129},{128,192},{129,65},{192,128},{193,2... | collective-permute-start | bytes 860168 | tf_op jit(solution)/shard_map/ppermute | solution.py:161
  25.8 16.6 %collective-permute-start.2 = (f32[80,896]{1,0:T(8,128)S(1)}, f32[80,896]{1,0:T(8,128)S(1)}, u32[]{:S(2)}, u32[]{:S(2)}) collective-permute-start(f32[80,896]{1,0:T(8,128)S(1)} %add.112), channel_id=1, source_target_pairs={{0,384},{1,129},{64,192},{65,449},{128,0},{129,257},{192,320},{193... | collective-permute-start | bytes 860168 | tf_op jit(solution)/shard_map/ppermute | solution.py:161
  36.6 7.7 %collective-permute-start.6 = (f32[80,896]{1,0:T(8,128)S(1)}, f32[80,896]{1,0:T(8,128)S(1)}, u32[]{:S(2)}, u32[]{:S(2)}) collective-permute-start(f32[80,896]{1,0:T(8,128)S(1)} %add_add_fusion), channel_id=1, source_target_pairs={{0,448},{1,65},{64,128},{65,1},{128,64},{129,193},{192,256},{193,1... | collective-permute-start | bytes 860168 | tf_op jit(solution)/shard_map/ppermute | solution.py:161
